TPU v7x, 256 devices: a whole 4x4x8 slice. The times are simulated.
256 devices in a mesh: store: 8 (over z), mp: 32 (over x, y, core).
Axes of the slice: x: 4, y: 4, z: 8, core: 2. Of those that a mesh axis runs over, the one named last changes fastest.
Arguments:
- kv_store: bfloat16 [128, 512, 2048], P('store', 'mp'), may hold values from -6 to 6
- retrieval: int32 [32, 8], replicated, may hold values from 0 to 127, as said below
- positions: int32 [32, 8], P('store'), may hold values from 0 to 7, each once within a row
- lengths: int32 [32], P('store'), may hold values from 1 to 128, 2048 in all
- queries: bfloat16 [32, 128, 8192], P('store', 'mp'), may hold values from -8 to 8
- new_kv: bfloat16 [32, 128, 2048], P('store', 'mp'), may hold values from -8 to 8
- hidden: bfloat16 [32, 128, 8192], P('store', 'mp'), may hold values from -4 to 4
- out_weight: bfloat16 [8192, 8192], P('mp'), may hold values from -0.0625 to 0.0625
- norm_gain: bfloat16 [8192], replicated, may hold values from 0.25 to 1.75
Outputs:
- residual_sum: bfloat16 [32, 128, 8192], P('store', 'mp')
- normed_out: bfloat16 [32, 128, 8192], P('store', 'mp')
Inputs may be any that keep to these rules, and one draw needn't show every extreme that they name: `retrieval`: store group of stretch c is c // 16. Taking the rows in consecutive blocks of 4 requests, the 32 ids of a block are all distinct and lie in exactly 4 store groups, 8 ids in each. `positions`: each row is a permutation of 0 to 7. `lengths`: they sum to 2048, and the largest is 128.
All inputs are finite; a program needn't handle non-finite values. No bound on the sum of `lengths` on one device may be relied on, other than what follows from the above.
Results may differ from a plain program's by a relative error of at most 0.015.
The roundings to bfloat16 on the way count: a program that leaves them out, or rounds other values in their place, can miss the bound.
Values may be sent and summed in bfloat16 or wider, within the bound.
A program may use at most 128 MiB of HBM per device.

v0:
```python
import jax
import jax.numpy as jnp
from jax import lax
from jax.sharding import PartitionSpec as P

KVH = 8
CTOK = 512
R = 8


theta_base = 1000000.0
eps_norm = 1e-06


def rotate(field_in, angles_at):
    half_dim = field_in.shape[-1] // 2
    inv_freq = theta_base ** (-(jnp.arange(half_dim, dtype=jnp.float32) * 2.0) / field_in.shape[-1])
    angles = angles_at[..., None] * inv_freq
    cosines = jnp.cos(angles)
    sine_val = jnp.sin(angles)
    lower_half = field_in[..., :half_dim]
    upper_half = field_in[..., half_dim:]
    return jnp.concatenate(
        [
            lower_half * cosines - upper_half * sine_val,
            upper_half * cosines + lower_half * sine_val,
        ],
        axis=-1,
    )


def on_device(
    kv_store, retrieval, positions, lengths, queries, new_kv, hidden, out_weight, norm_gain
):
    stores = lax.axis_size("store")
    shards = lax.axis_size("mp")
    group_id = lax.axis_index("store")
    device_pos = lax.axis_index("mp")
    req_here = positions.shape[0]
    slots_here = req_here * R
    slab_tok = kv_store.shape[1]
    row_width = kv_store.shape[2]
    all_ids = retrieval.reshape(stores, slots_here)
    own_ids = lax.dynamic_index_in_dim(all_ids, group_id, 0, keepdims=False)
    empty_rows = jnp.zeros((slots_here, slab_tok, row_width), kv_store.dtype)
    block_rows = lax.all_gather(kv_store, "store", axis=0, tiled=True)
    row_count = block_rows.shape[0]
    inside = (own_ids >= 0) & (own_ids < row_count)
    picked = jnp.take(block_rows, jnp.clip(own_ids, 0, row_count - 1), axis=0)
    fetched = jnp.where(inside[:, None, None], picked, empty_rows)
    repeat_count = shards // KVH
    width_pair = row_width // KVH
    head_dim = width_pair // 2
    query_rows = new_kv.shape[1]
    query_len = query_rows * shards
    context = R * CTOK
    heads_total = queries.shape[2] // head_dim
    heads_here = heads_total // shards
    own_tokens = device_pos * query_rows + jnp.arange(query_rows, dtype=jnp.int32)
    own_places = (context + own_tokens).astype(jnp.float32)
    rot_query = rotate(
        queries.reshape(req_here, query_rows, heads_total, head_dim).astype(jnp.float32),
        own_places[None, :, None],
    ).astype(jnp.bfloat16)
    stretch_send = jnp.repeat(
        fetched.reshape(slots_here, slab_tok, KVH, width_pair), repeat_count, axis=2
    )
    fresh_send = jnp.repeat(
        new_kv.reshape(req_here, query_rows, KVH, width_pair), repeat_count, axis=2
    )
    query_send = rot_query.reshape(req_here, query_rows, shards, heads_here * head_dim)
    stretch_head, fresh_head, query_head = (
        lax.all_to_all(stretch_send, "mp", split_axis=2, concat_axis=1, tiled=True),
        lax.all_to_all(fresh_send, "mp", split_axis=2, concat_axis=1, tiled=True),
        lax.all_to_all(query_send, "mp", split_axis=2, concat_axis=1, tiled=True),
    )
    fresh_order = jnp.arange(query_len, dtype=jnp.int32)
    query_head = query_head.reshape(req_here, query_len, heads_here, head_dim)
    stretch_head = stretch_head.reshape(req_here, R, -1, 2, head_dim)
    offsets = (positions * CTOK).astype(jnp.float32)
    stretch_keys = rotate(stretch_head[:, :, :, 0].astype(jnp.float32), offsets[:, :, None]).astype(
        jnp.bfloat16
    )
    stretch_keys = stretch_keys.reshape(req_here, -1, head_dim)
    stretch_values = stretch_head[:, :, :, 1].reshape(req_here, -1, head_dim)
    stretch_count = stretch_keys.shape[1]
    fresh_head = fresh_head.reshape(req_here, -1, 2, head_dim)
    fresh_places = (context + fresh_order).astype(jnp.float32)
    own_keys = rotate(fresh_head[:, :, 0].astype(jnp.float32), fresh_places[None, :]).astype(
        jnp.bfloat16
    )
    all_keys = jnp.concatenate([stretch_keys, own_keys], axis=1)
    values = jnp.concatenate([stretch_values, fresh_head[:, :, 1]], axis=1)
    token_index = jnp.arange(query_len, dtype=jnp.int32)
    own_allowed = fresh_order[None, :] <= token_index[:, None]
    allowed = jnp.concatenate([jnp.ones((query_len, stretch_count), bool), own_allowed], axis=1)
    scores = jnp.einsum(
        "bthd,bsd->bhts", query_head, all_keys, preferred_element_type=jnp.float32
    ) * head_dim ** (-0.5)
    scores = jnp.where(allowed[None, None], scores, -1e30)
    highest = jnp.max(scores, axis=-1, keepdims=True)
    exponent = jnp.where(allowed[None, None], jnp.exp(scores - highest), 0.0)
    row_total = jnp.sum(exponent, axis=-1, keepdims=True)
    weights = exponent.astype(jnp.bfloat16)
    value_sums = jnp.einsum("bhts,bsd->bhtd", weights, values, preferred_element_type=jnp.float32)
    blended = value_sums / row_total
    blended = jnp.transpose(blended, (0, 2, 1, 3)).reshape(
        req_here, query_len, heads_here * head_dim
    )
    blended = jnp.where((token_index[None, :] < lengths[:, None])[:, :, None], blended, 0.0)
    attended = blended.astype(jnp.bfloat16)
    by_token = jnp.transpose(attended, (1, 0, 2))
    summed = lax.psum_scatter(
        jnp.einsum("tbc,cd->tbd", by_token, out_weight, preferred_element_type=jnp.float32).astype(
            jnp.bfloat16
        ),
        "mp",
        scatter_dimension=0,
        tiled=True,
    ).astype(jnp.float32)
    mixed = hidden.astype(jnp.float32) + jnp.transpose(summed, (1, 0, 2))
    residual_sum = mixed.astype(jnp.bfloat16)
    normed = (
        mixed
        * lax.rsqrt(jnp.mean(mixed * mixed, axis=-1, keepdims=True) + eps_norm)
        * norm_gain.astype(jnp.float32)
    )
    return (residual_sum, normed.astype(jnp.bfloat16))


def solution(mesh):
    return jax.shard_map(
        on_device,
        mesh=mesh,
        in_specs=(
            P("store", "mp", None),
            P(),
            P("store", None),
            P("store"),
            P("store", "mp", None),
            P("store", "mp", None),
            P("store", "mp", None),
            P("mp", None),
            P(),
        ),
        out_specs=(P("store", "mp", None), P("store", "mp", None)),
        check_vma=False,
    )
```

profile of v0, /device:TPU:1, one launch (start us, length us, event | category | flops | bytes accessed | tf_op | source)
XLA Modules:
  0.0 505.1 jit_solution(16870470741391214173)
XLA Ops:
  7.2 0.7 all-gather.2.cloned.1.call-update
  7.9 0.9 copy.64
  8.8 0.8 broadcast_in_dim.80
  9.6 8.6 %all-to-all-start.1 = ((bf16[4,4,32,256]{3,1,0,2:T(4,128)(2,1)}), bf16[4,4,32,256]{3,1,0,2:T(4,128)(2,1)S(1)}, u32[]{:S(2)}, u32[]{:S(2)}) async-start(bf16[4,4,32,256]{3,1,0,2:T(4,128)(2,1)} %bitcast.10), calls=%async_computation.1 | async-start | bytes 524288 | tf_op jit(solution)/shard_map/all_to_all | solution.py:74
  18.2 0.8 copy.34
  18.9 0.1 reshape.276
  19.0 1.2 reshape.286
  20.2 0.1 multiply_cosine_fusion.2
  20.3 0.2 subtract_convert_fusion.1
  20.6 0.2 pad_maximum_fusion
  20.8 0.1 convert_element_type.81
  20.9 0.9 copy.40
  21.8 86.0 %all-gather.2.cloned.1.call-done = bf16[128,16,2048]{2,1,0:T(8,128)(2,1)} async-done(((bf16[16,16,2048]{2,1,0:T(8,128)(2,1)}), bf16[128,16,2048]{2,1,0:T(8,128)(2,1)}) %all-gather.2.cloned.1.call-update) | async-done | bytes 8388624 | tf_op jit(solution)/shard_map/all_gather | solution.py:46
  107.8 5.4 %gather_fusion = bf16[32,16,2048]{2,1,0:T(8,128)(2,1)} fusion(bf16[128,16,2048]{2,1,0:T(8,128)(2,1)} %all-gather.2.cloned.1.call-done, s32[1024]{0:T(1024)S(1)} %pad_clamp_fusion), kind=kCustom, calls=%fused_computation | custom fusion | bytes 4194432 | tf_op jit(solution)/shard_map/jit(_take)/gather | solution.py:49
  113.2 2.3 copy.57
  115.5 7.5 %all-to-all-start.2 = ((bf16[4,4,32,256]{3,1,0,2:T(4,128)(2,1)}), bf16[4,4,32,256]{3,1,0,2:T(4,128)(2,1)S(1)}, u32[]{:S(2)}, u32[]{:S(2)}) async-start(bf16[4,4,32,256]{3,1,0,2:T(4,128)(2,1)} %copy.40), calls=%async_computation.2 | async-start | bytes 524288 | tf_op jit(solution)/shard_map/all_to_all | solution.py:75
  123.0 0.3 fusion.17
  123.4 0.4 copy.35
  123.8 8.2 %all-to-all-done.2 = bf16[4,4,32,256]{3,1,0,2:T(4,128)(2,1)S(1)} async-done(((bf16[4,4,32,256]{3,1,0,2:T(4,128)(2,1)}), bf16[4,4,32,256]{3,1,0,2:T(4,128)(2,1)S(1)}, u32[]{:S(2)}, u32[]{:S(2)}) %all-to-all-start.2) | async-done | bytes 262176 | tf_op jit(solution)/shard_map/all_to_all | solution.py:75
  132.0 4.2 broadcast_in_dim.79
  136.2 4.9 all-to-all-start
  141.1 0.2 all-reduce.4.cloned.1.call-start
  141.4 0.1 concatenate.26
  141.6 0.1 multiply_cosine_fusion.1
  141.8 0.3 multiply_cosine_fusion
  142.1 0.1 copy.38
  142.2 0.1 reshape.281
  142.3 0.4 fusion.38
  142.7 0.1 copy.54
  142.8 0.1 copy.41
  142.9 0.1 reshape.282
  143.0 0.1 subtract_convert_fusion.2
  143.2 104.7 %all-to-all-done = bf16[32,16,32,256]{3,1,0,2:T(8,128)(2,1)} async-done(((bf16[32,16,32,256]{3,1,0,2:T(8,128)(2,1)}), bf16[32,16,32,256]{3,1,0,2:T(8,128)(2,1)}, u32[]{:S(2)}, u32[]{:S(2)}) %all-to-all-start) | async-done | bytes 8388640 | tf_op jit(solution)/shard_map/all_to_all | solution.py:73
  247.9 7.7 %copy.36 = bf16[32,32,16,1,256]{4,2,1,0,3:T(8,128)(2,1)} copy(bf16[32,32,16,1,256]{4,2,0,1,3:T(8,128)(2,1)} %bitcast.6) | data formatting | bytes 16777216 | tf_op jit(solution)/shard_map/all_to_all | solution.py:73
  255.6 12.6 %reshape.278 = bf16[4,8,512,2,128]{4,3,2,1,0:T(2,128)(2,1)} reshape(bf16[32,32,16,1,256]{4,2,1,0,3:T(8,128)(2,1)} %copy.36) | data formatting | bytes 16777216 | tf_op jit(solution)/shard_map/reshape | solution.py:79
  268.2 17.4 %fusion.37 = (bf16[4,8,512,1,128]{4,3,2,1,0:T(2,128)(2,1)S(1)}, f32[4,8,512,1,128]{4,3,2,1,0:T(1,128)}) fusion(bf16[4,8,512,2,128]{4,3,2,1,0:T(2,128)(2,1)} %reshape.278), kind=kLoop, calls=%fused_computation.72 | loop fusion | flops 2097152 | bytes 20971520 | tf_op jit(solution)/shard_map/slice | solution.py:85
  285.6 2.6 copy.53
  288.2 6.5 %copy.50 = bf16[4,4096,128]{1,2,0:T(8,128)(2,1)} copy(bf16[4,4096,128]{2,1,0:T(8,128)(2,1)} %bitcast.96) | data formatting | bytes 8388608 | tf_op jit(solution)/shard_map/reshape;squeeze | solution.py:85
  294.7 10.7 %subtract_convert_fusion = (bf16[4,8,512,64]{3,2,1,0:T(8,128)(2,1)}, bf16[4,8,512,64]{3,2,1,0:T(8,128)(2,1)}) fusion(f32[4,8,512,128]{3,2,1,0:T(8,128)} %bitcast.94, f32[4,8,64]{2,1,0:T(8,128)S(1)} %get-tuple-element.15, f32[4,8,64]{2,1,0:T(8,128)S(1)} %get-tuple-element.14), kind=kLoop, calls=%fused_computation.13 | loop fusion | flops 8388608 | bytes 12599296 | tf_op jit(solution)/shard_map/convert.11
  305.4 10.0 %fusion.9 = f32[4,4224,128,2]{2,1,3,0:T(8,128)} fusion(bf16[4,128,64]{2,1,0:T(8,128)(2,1)S(1)} %get-tuple-element.11, bf16[4,128,64]{2,1,0:T(8,128)(2,1)S(1)} %get-tuple-element.10, bf16[4,4096,64]{2,1,0:T(8,128)(2,1)} %bitcast.98, bf16[4,4096,64]{2,1,0:T(8,128)(2,1)} %bitcast.97, bf16[4,128,2,128]{3,2,1,0:T(2,128)(2,1)S(1)} %reshape.282), kind=kOutput, calls=%fused_computation.18 | convolution fusion | flops 1124597760 | bytes 21889024 | tf_op jit(solution)/shard_map/bthd,bsd->bhts/dot_general | solution.py:97
  315.5 24.1 %fusion.39 = (f32[4,2,128]{2,1,0:T(2,128)S(1)}, bf16[4,2,128,4224]{2,3,1,0:T(8,128)(2,1)S(1)}) fusion(f32[4,4224,128,2]{2,1,3,0:T(8,128)} %fusion.9, pred[128,4224]{0,1:T(8,128)(4,1)S(1)} %concatenate.26), kind=kOutput, calls=%fused_computation.74 | output fusion | flops 25956480 | bytes 26497024 | tf_op jit(solution)/shard_map/sub | solution.py:102
  339.6 1.4 fusion.21
  341.1 0.1 copy.46
  341.2 7.9 %convolution_convert_fusion = bf16[128,4,8192]{2,0,1:T(8,128)(2,1)} fusion(bf16[256,8192]{1,0:T(8,128)(2,1)} %param.16, bf16[4,128,256]{2,1,0:T(8,128)(2,1)S(1)} %copy.46, pred[4,128]{1,0:T(4,128)(4,1)S(1)} %iota_compare_fusion.1), kind=kOutput, calls=%fused_computation.5 | convolution fusion | flops 2151809024 | bytes 12845568 | tf_op jit(solution)/shard_map/tbc,cd->tbd/dot_general | solution.py:114
  349.2 0.6 dynamic-slice
  350.4 144.3 %all-reduce.4.cloned.1.call-done = bf16[128,4,8192]{2,0,1:T(8,128)(2,1)} async-done(((bf16[128,4,8192]{2,0,1:T(8,128)(2,1)}), bf16[128,4,8192]{2,0,1:T(8,128)(2,1)}) %all-reduce.4.cloned.1.call-update) | async-done | bytes 8388624
  494.7 1.4 multiply_reduce_fusion
  496.1 2.1 multiply_convert_fusion
  (28 shorter events, 0.3 us)
Async XLA Ops:
  7.2 100.6 %all-gather.2.cloned.1.call-start = ((), (), s32[]{:S(2)}) async-start(), calls=%async_computation.3 | async-start | bytes 9437184 | tf_op jit(solution)/shard_map/all_gather | solution.py:46
  9.6 105.9 %all-to-all-start.1 = ((bf16[4,4,32,256]{3,1,0,2:T(4,128)(2,1)}), bf16[4,4,32,256]{3,1,0,2:T(4,128)(2,1)S(1)}, u32[]{:S(2)}, u32[]{:S(2)}) async-start(bf16[4,4,32,256]{3,1,0,2:T(4,128)(2,1)} %bitcast.10), calls=%async_computation.1 | async-start | bytes 524288 | tf_op jit(solution)/shard_map/all_to_all | solution.py:74
  115.5 16.5 %all-to-all-start.2 = ((bf16[4,4,32,256]{3,1,0,2:T(4,128)(2,1)}), bf16[4,4,32,256]{3,1,0,2:T(4,128)(2,1)S(1)}, u32[]{:S(2)}, u32[]{:S(2)}) async-start(bf16[4,4,32,256]{3,1,0,2:T(4,128)(2,1)} %copy.40), calls=%async_computation.2 | async-start | bytes 524288 | tf_op jit(solution)/shard_map/all_to_all | solution.py:75
  136.2 5.3 %copy-start.4 = (s32[4]{0:T(128)S(1)}, s32[4]{0:T(128)}, u32[]{:S(2)}) copy-start(s32[4]{0:T(128)} %param.12) | copy-start | bytes 52
  136.2 5.4 %copy-start.3 = (s32[4,8]{1,0:T(4,128)S(1)}, s32[4,8]{1,0:T(4,128)}, u32[]{:S(2)}) copy-start(s32[4,8]{1,0:T(4,128)} %param.11) | copy-start | bytes 388
  136.2 111.7 %all-to-all-start = ((bf16[32,16,32,256]{3,1,0,2:T(8,128)(2,1)}), bf16[32,16,32,256]{3,1,0,2:T(8,128)(2,1)}, u32[]{:S(2)}, u32[]{:S(2)}) async-start(bf16[32,16,32,256]{3,1,0,2:T(8,128)(2,1)} %bitcast.95), calls=%async_computation | async-start | bytes 16777216 | tf_op jit(solution)/shard_map/all_to_all | solution.py:73
  141.1 353.6 %all-reduce.4.cloned.1.call-start = ((), (), s32[]{:S(2)}) async-start(), calls=%async_computation.4 | async-start | bytes 16777216
  315.5 24.2 %copy-start = (bf16[4,4096,128]{1,2,0:T(8,128)(2,1)S(1)}, bf16[4,4096,128]{1,2,0:T(8,128)(2,1)}, u32[]{:S(2)}) copy-start(bf16[4,4096,128]{1,2,0:T(8,128)(2,1)} %copy.50) | copy-start | bytes 12582916
  341.2 7.9 %copy-start.2 = (bf16[8192]{0:T(1024)(128)(2,1)S(1)}, bf16[8192]{0:T(1024)(128)(2,1)}, u32[]{:S(2)}) copy-start(bf16[8192]{0:T(1024)(128)(2,1)} %param.17) | copy-start | bytes 49156
  341.2 8.0 %copy-start.5 = (u32[256]{0:T(256)S(1)}, u32[256]{0:T(256)}, u32[]{:S(2)}) copy-start(u32[256]{0:T(256)} %constant.75) | copy-start | bytes 3076
  341.2 153.5 %copy-start.1 = (bf16[4,4,8192]{2,1,0:T(4,128)(2,1)S(1)}, bf16[4,4,8192]{2,1,0:T(4,128)(2,1)}, u32[]{:S(2)}) copy-start(bf16[4,4,8192]{2,1,0:T(4,128)(2,1)} %param.15) | copy-start | bytes 786436
Sparse Core Ops, SparseCore 0:
  9.8 97.9 all-gather.1
  349.3 145.4 all-reduce.3
where the time goes:
time: 506 us; the launch traced here: 505 us
  waiting for transfers between devices  344 us (68%)
  other arithmetic  57.5 us (11%)
  local copies, waits for them, and re-layouts  48.2 us (10%)
  starting transfers between devices  21.3 us (4%)
  matrix products  19.3 us (4%)
  between operations  15 us (3%)
    unnamed x3, waiting for transfers between devices  145 us
    all_to_all x1, waiting for transfers between devices, on_device(): lax.all_to_all(stretch_send, 'mp', split_axis=2, concat_axis=1, tiled=True)  105 us
    all_gather x1, waiting for transfers between devices, on_device(): block_rows = lax.all_gather(kv_store, 'store', axis=0, tiled=True)  86 us
    sub x1, other arithmetic, on_device(): exponent = jnp.where(allowed[None, None], jnp.exp(scores - highest), 0.0)  24.1 us
    slice x1, other arithmetic, on_device(): stretch_values = stretch_head[:, :, :, 1].reshape(req_here, -1, head_dim)  17.4 us
    reshape x1, local copies, waits for them, and re-layouts, on_device(): stretch_head = stretch_head.reshape(req_here, R, -1, 2, head_dim)  12.6 us
    another operation x3, other arithmetic  11.1 us
  transfers between devices with their start and end apart: 5, of which 4 were waited for; matrix products, arithmetic and copies ran while one was open for 3% of the time, Pallas kernels for 0%

commit v1 on v0

v1 whole, which is shorter than its diff:
```python
import jax
import jax.numpy as jnp
import numpy as np
from jax import lax
from jax.experimental import pallas as pl
from jax.experimental.pallas import tpu as pltpu
from jax.sharding import PartitionSpec as P

MESH = pl.DeviceIdType.MESH
ANY = pl.BlockSpec(memory_space=pl.ANY)
VMEM = pl.BlockSpec(memory_space=pltpu.VMEM)
SMEM = pl.BlockSpec(memory_space=pltpu.SMEM)

STORES = 8
SHARDS = 32
HEADS = 64
KVH = 8
GROUP = 8
HD = 128
D = 8192
QUARTERS = 4
CTOK = 512
R = 8
REQ = 4
QMAX = 128
HELD = 16
CHUNKS = 4
PER = HELD // CHUNKS
WIDTH = D // QUARTERS
ROWS = QMAX * GROUP
LANES = 256

theta_base = 1000000.0
eps_norm = 1e-06


def turns(places):
    inv_freq = theta_base ** (-(jnp.arange(HD // 2, dtype=jnp.float32) * 2.0) / HD)
    angles = places[..., None] * inv_freq
    cosines, sines = jnp.cos(angles), jnp.sin(angles)
    return (
        jnp.concatenate([cosines, cosines], axis=-1),
        jnp.concatenate([-sines, sines], axis=-1),
    )


def rotate(field_in, cosines, sines):
    half = HD // 2
    other = jnp.concatenate([field_in[..., half:], field_in[..., :half]], axis=-1)
    return field_in * cosines + other * sines


def ahead(a, b, n):
    return lax.rem(a + b, n)


def spread_kernel(
    kv, q, fresh, w, kv_all, q_all, fresh_all, w_all,
    own_sem, kv_send, kv_recv, q_send, q_recv, f_send, f_recv, w_send, w_recv, z_send, z_recv,
):
    m = lax.axis_index("mp")
    z = lax.axis_index("store")
    k = m // QUARTERS
    j = lax.rem(m, QUARTERS)
    right, left = ahead(z, 1, STORES), ahead(z, STORES - 1, STORES)

    barrier = pltpu.get_barrier_semaphore()

    def greet(i, carry):
        pl.semaphore_signal(barrier, 1, device_id={"mp": ahead(m, i, SHARDS)}, device_id_type=MESH)
        return carry

    lax.fori_loop(1, SHARDS, greet, 0)
    for near in (left, right):
        pl.semaphore_signal(barrier, 1, device_id={"store": near}, device_id_type=MESH)
    pl.semaphore_wait(barrier, SHARDS + 1)

    def remote(src, dst, send, recv, **where):
        return pltpu.make_async_remote_copy(
            src_ref=src, dst_ref=dst, send_sem=send, recv_sem=recv, device_id=where, device_id_type=MESH
        )

    def kv_rows(c, head):
        return kv_all.at[z, pl.ds(PER * c, PER), pl.ds(pl.multiple_of(16 * head, 16), 16), :]

    def kv_part(c, head):
        return kv.at[pl.ds(PER * c, PER), :, pl.ds(pl.multiple_of(2 * HD * head, 2 * HD), 2 * HD)]

    def kv_copy(c, i):
        to = ahead(k, i, KVH)
        return remote(
            kv_part(c, to), kv_rows(c, k), kv_send.at[c, i], kv_recv.at[c, k], mp=QUARTERS * to + j
        )

    def kv_arrival(c, i):
        come = ahead(k, i, KVH)
        return remote(
            kv_part(c, come), kv_rows(c, come), kv_send.at[c, i], kv_recv.at[c, come], mp=QUARTERS * come + j
        )

    def own_kv(c):
        return pltpu.make_async_copy(kv_part(c, k), kv_rows(c, k), own_sem.at[c])

    for c in range(CHUNKS):
        own_kv(c).start()

        def send_kv(i, carry):
            kv_copy(c, i).start()
            return carry

        lax.fori_loop(1, KVH, send_kv, 0)

    def z_copy(way, s, c):
        owner = ahead(z, (STORES - s) if way == 0 else s, STORES)
        slab = kv_all.at[owner, pl.ds(PER * c, PER)]
        return remote(
            slab, slab, z_send.at[way, s, c], z_recv.at[way, s, c], store=right if way == 0 else left
        )

    def z_arrival(way, s, c):
        owner = ahead(z, (STORES - 1 - s) if way == 0 else (s + 1), STORES)
        slab = kv_all.at[owner, pl.ds(PER * c, PER)]
        return remote(
            slab, slab, z_send.at[way, s, c], z_recv.at[way, s, c], store=right if way == 0 else left
        )

    for c in range(CHUNKS):
        own_kv(c).wait()

        def take_kv(i, carry):
            kv_arrival(c, i).wait_recv()
            return carry

        lax.fori_loop(1, KVH, take_kv, 0)
        for way in range(2):
            z_copy(way, 0, c).start()

    def fresh_part(head):
        return fresh.at[:, pl.ds(pl.multiple_of(2 * HD * head, 2 * HD), 2 * HD)]

    def f_copy(i):
        to = ahead(k, i, KVH)
        return remote(fresh_part(to), fresh_all.at[k], f_send.at[i], f_recv.at[k], mp=QUARTERS * to + j)

    def f_arrival(i):
        come = ahead(k, i, KVH)
        return remote(fresh_part(come), fresh_all.at[come], f_send.at[i], f_recv.at[come], mp=QUARTERS * come + j)

    def q_copy(i):
        to = ahead(m, i, SHARDS)
        return remote(q.at[to // QUARTERS], q_all.at[:, m], q_send.at[i], q_recv.at[m], mp=to)

    def q_arrival(i):
        come = ahead(m, i, SHARDS)
        return remote(q.at[k], q_all.at[:, come], q_send.at[i], q_recv.at[come], mp=come)

    def w_part(block):
        return w.at[:, pl.ds(pl.multiple_of(WIDTH * block, WIDTH), WIDTH)]

    def w_copy(i):
        to = ahead(j, i, QUARTERS)
        return remote(w_part(to), w_all.at[j], w_send.at[i], w_recv.at[j], mp=QUARTERS * k + to)

    def w_arrival(i):
        come = ahead(j, i, QUARTERS)
        return remote(w_part(come), w_all.at[come], w_send.at[i], w_recv.at[come], mp=QUARTERS * k + come)

    own = [
        pltpu.make_async_copy(fresh_part(k), fresh_all.at[k], own_sem.at[CHUNKS]),
        pltpu.make_async_copy(q.at[k], q_all.at[:, m], own_sem.at[CHUNKS + 1]),
        pltpu.make_async_copy(w_part(j), w_all.at[j], own_sem.at[CHUNKS + 2]),
    ]

    def loop(low, high, act):
        def body(i, carry):
            act(i)
            return carry

        lax.fori_loop(low, high, body, 0)

    for copy in own:
        copy.start()
    loop(1, QUARTERS, lambda i: w_copy(i).start())
    loop(1, KVH, lambda i: f_copy(i).start())
    loop(1, SHARDS, lambda i: q_copy(i).start())

    last = STORES // 2 - 1
    halves = (range(CHUNKS // 2), range(CHUNKS // 2, CHUNKS))
    for s in range(1, last + 1):
        for c in range(CHUNKS):
            for way in range(2):
                if s < last or c in halves[way]:
                    z_arrival(way, s - 1, c).wait_recv()
                    z_copy(way, s, c).start()
    for way in range(2):
        for c in range(CHUNKS):
            if c in halves[way]:
                z_arrival(way, last, c).wait_recv()
            else:
                z_arrival(way, last - 1, c).wait_recv()

    for copy in own:
        copy.wait()
    loop(1, QUARTERS, lambda i: w_arrival(i).wait_recv())
    loop(1, KVH, lambda i: f_arrival(i).wait_recv())
    loop(1, SHARDS, lambda i: q_arrival(i).wait_recv())
    loop(1, QUARTERS, lambda i: w_copy(i).wait_send())
    loop(1, KVH, lambda i: f_copy(i).wait_send())
    loop(1, SHARDS, lambda i: q_copy(i).wait_send())
    for c in range(CHUNKS):
        loop(1, KVH, lambda i: kv_copy(c, i).wait_send())
    for way in range(2):
        for s in range(last + 1):
            for c in range(CHUNKS):
                if s < last or c in halves[way]:
                    z_copy(way, s, c).wait_send()


def spread(kv, q, fresh, w):
    bf = jnp.bfloat16
    dma = pltpu.SemaphoreType.DMA
    return pl.pallas_call(
        spread_kernel,
        out_shape=(
            jax.ShapeDtypeStruct((STORES, HELD, CTOK // QUARTERS, 2 * HD), bf),
            jax.ShapeDtypeStruct((REQ, SHARDS, QMAX // SHARDS * GROUP, HD), bf),
            jax.ShapeDtypeStruct((KVH, 16, 2 * HD), bf),
            jax.ShapeDtypeStruct((QUARTERS, D // SHARDS, WIDTH), bf),
        ),
        in_specs=[ANY] * 4,
        out_specs=(ANY,) * 4,
        scratch_shapes=[
            dma((CHUNKS + 3,)),
            dma((CHUNKS, KVH)), dma((CHUNKS, KVH)),
            dma((SHARDS,)), dma((SHARDS,)),
            dma((KVH,)), dma((KVH,)),
            dma((QUARTERS,)), dma((QUARTERS,)),
            dma((2, STORES // 2, CHUNKS)), dma((2, STORES // 2, CHUNKS)),
        ],
        compiler_params=pltpu.CompilerParams(collective_id=0, has_side_effects=True),
        name="spread",
    )(kv, q, fresh, w)


def attend_kernel(
    ids, places, lengths, q, fresh, cosines, sines, kv_all, out, lse, slots, keys, values, sem
):
    quarter = CTOK // QUARTERS
    j = lax.rem(lax.axis_index("mp"), QUARTERS)

    def fetch(n):
        return pltpu.make_async_copy(kv_all.at[ids[n]], slots.at[n], sem.at[n])

    for n in range(REQ * R):
        fetch(n).start()
    keys[R * quarter :, :] = fresh[:, :HD]
    values[:, R * quarter :] = fresh[:, HD:].astype(jnp.float32).T.astype(jnp.bfloat16)
    row = lax.broadcasted_iota(jnp.int32, (quarter, LANES), 0)
    lane = lax.broadcasted_iota(jnp.int32, (quarter, LANES), 1)
    fresh_token = 4 * (QUARTERS * (row >> 4) + j) + (row & 3)
    fresh_request = (row >> 2) & 3
    for b in range(REQ):
        for r in range(R):
            n = b * R + r
            fetch(n).wait()
            key = slots[n, :, :HD].astype(jnp.float32)
            at = places[n]
            key = key * cosines[pl.ds(at, 1), :] + pltpu.roll(key, HD // 2, 1) * sines[pl.ds(at, 1), :]
            keys[r * quarter : (r + 1) * quarter, :] = key.astype(jnp.bfloat16)
            values[:, r * quarter : (r + 1) * quarter] = (
                slots[n, :, HD:].astype(jnp.float32).T.astype(jnp.bfloat16)
            )
        length = lengths[b]

        def block(i, carry):
            span = pl.ds(pl.multiple_of(i * LANES, LANES), LANES)

            @pl.when(i * LANES < length * GROUP)
            def _():
                scores = lax.dot_general(
                    keys[...], q[b, span, :], (((1,), (1,)), ((), ())), preferred_element_type=jnp.float32
                ) * (HD**-0.5)
                token = (i * LANES + lane) >> 3
                allowed = (fresh_request == b) & (fresh_token <= token)
                scores = jnp.concatenate(
                    [scores[: R * quarter], jnp.where(allowed, scores[R * quarter :], -1e30)], axis=0
                )
                top = jnp.max(scores, axis=0, keepdims=True)
                expo = jnp.exp(scores - top)
                total = jnp.sum(expo, axis=0, keepdims=True)
                sums = jnp.dot(
                    values[...], expo.astype(jnp.bfloat16), preferred_element_type=jnp.float32
                )
                used = (i * LANES + lane) < length * GROUP
                out[b, :, span] = jnp.where(used, sums / total, 0.0).astype(jnp.bfloat16)
                lse[b, :, span] = jnp.broadcast_to(top + jnp.log(total), (8, LANES))

            @pl.when(i * LANES >= length * GROUP)
            def _():
                out[b, :, span] = jnp.zeros((HD, LANES), jnp.bfloat16)
                lse[b, :, span] = jnp.zeros((8, LANES), jnp.float32)

            return carry

        lax.fori_loop(0, ROWS // LANES, block, 0)


def attend(ids, places, lengths, q, fresh, cosines, sines, kv_all):
    quarter = CTOK // QUARTERS
    return pl.pallas_call(
        attend_kernel,
        out_shape=(
            jax.ShapeDtypeStruct((REQ, HD, ROWS), jnp.bfloat16),
            jax.ShapeDtypeStruct((REQ, 8, ROWS), jnp.float32),
        ),
        in_specs=[SMEM] * 3 + [VMEM] * 4 + [ANY],
        out_specs=(VMEM, VMEM),
        scratch_shapes=[
            pltpu.VMEM((REQ * R, quarter, 2 * HD), jnp.bfloat16),
            pltpu.VMEM(((R + 1) * quarter, HD), jnp.bfloat16),
            pltpu.VMEM((HD, (R + 1) * quarter), jnp.bfloat16),
            pltpu.SemaphoreType.DMA((REQ * R,)),
        ],
        compiler_params=pltpu.CompilerParams(vmem_limit_bytes=32 << 20),
        name="attend",
    )(ids, places, lengths, q, fresh, cosines, sines, kv_all)


def merge_kernel(
    part, lse, w_hbm, hidden, gain, residual, normed,
    w, got_part, got_lse, rows, attended, sent, got, mixed,
    w_sem, own_sem, c_send, c_recv, l_send, l_recv, g_send, g_recv, p_send, p_recv,
):
    m = lax.axis_index("mp")
    k = m // QUARTERS
    j = lax.rem(m, QUARTERS)
    w_load = pltpu.make_async_copy(w_hbm, w, w_sem)
    w_load.start()

    barrier = pltpu.get_barrier_semaphore()

    def loop(low, high, act):
        def body(i, carry):
            act(i)
            return carry

        lax.fori_loop(low, high, body, 0)

    loop(
        1,
        SHARDS,
        lambda i: pl.semaphore_signal(
            barrier, 1, device_id={"mp": ahead(m, i, SHARDS)}, device_id_type=MESH
        ),
    )
    pl.semaphore_wait(barrier, SHARDS - 1)

    def remote(src, dst, send, recv, to):
        return pltpu.make_async_remote_copy(
            src_ref=src, dst_ref=dst, send_sem=send, recv_sem=recv, device_id={"mp": to}, device_id_type=MESH
        )

    def part_copy(i):
        to = ahead(j, i, QUARTERS)
        return remote(part.at[to], got_part.at[i], c_send.at[i], c_recv.at[i], QUARTERS * k + to)

    def lse_copy(i):
        to = ahead(j, i, QUARTERS)
        return remote(lse.at[to], got_lse.at[i], l_send.at[i], l_recv.at[i], QUARTERS * k + to)

    for i in range(1, QUARTERS):
        lse_copy(i).start()
        part_copy(i).start()
    for i in range(1, QUARTERS):
        lse_copy(i).wait_recv()
    logs = [lse[j, :1, :]] + [got_lse[i, :1, :] for i in range(1, QUARTERS)]
    top = jnp.maximum(jnp.maximum(logs[0], logs[1]), jnp.maximum(logs[2], logs[3]))
    shares = [jnp.exp(one - top) for one in logs]
    scale = 1.0 / (shares[0] + shares[1] + shares[2] + shares[3])
    total = part[j].astype(jnp.float32) * (shares[0] * scale)
    for i in range(1, QUARTERS):
        part_copy(i).wait_recv()
        total = total + got_part[i].astype(jnp.float32) * (shares[i] * scale)
    rows[...] = total.T
    for h in range(GROUP):
        attended[j, :, h * HD : (h + 1) * HD] = rows[pl.ds(h, QMAX, stride=GROUP), :].astype(jnp.bfloat16)

    def g_copy(i):
        to = ahead(j, i, QUARTERS)
        return remote(attended.at[j], attended.at[j], g_send.at[i], g_recv.at[j], QUARTERS * k + to)

    def g_arrival(i):
        come = ahead(j, i, QUARTERS)
        return remote(attended.at[come], attended.at[come], g_send.at[i], g_recv.at[come], QUARTERS * k + come)

    for i in range(1, QUARTERS):
        g_copy(i).start()
    w_load.wait()
    for i in range(1, QUARTERS):
        g_arrival(i).wait_recv()

    tokens = QMAX // SHARDS
    owned = REQ * tokens
    span = REQ * QMAX // 4
    per = span // owned

    def p_copy(to):
        return remote(
            sent.at[pl.ds(pl.multiple_of(owned * to, owned), owned), :], got.at[m], p_send.at[to], p_recv.at[m], to
        )

    def p_own():
        return pltpu.make_async_copy(
            sent.at[pl.ds(pl.multiple_of(owned * m, owned), owned), :], got.at[m], own_sem
        )

    def p_arrival(come):
        return remote(
            sent.at[pl.ds(pl.multiple_of(owned * come, owned), owned), :], got.at[come], p_send.at[come], p_recv.at[come], come
        )

    def project(i):
        block = ahead(m // per, i, 4)
        at = block * span + lax.broadcasted_iota(jnp.int32, (span, REQ * QMAX), 0)
        source = QMAX * ((at >> 2) & 3) + 4 * (at >> 4) + (at & 3)
        pick = (source == lax.broadcasted_iota(jnp.int32, (span, REQ * QMAX), 1)).astype(jnp.bfloat16)
        chosen = jnp.dot(
            pick, attended[...].reshape(REQ * QMAX, GROUP * HD), preferred_element_type=jnp.float32
        ).astype(jnp.bfloat16)
        sent[pl.ds(pl.multiple_of(block * span, span), span), :] = jnp.dot(
            chosen, w[...].reshape(GROUP * HD, WIDTH), preferred_element_type=jnp.float32
        ).astype(jnp.bfloat16)

        def ship(t):
            to = block * per + ahead(m, t, per)

            @pl.when(to != m)
            def _():
                p_copy(to).start()

            @pl.when(to == m)
            def _():
                p_own().start()

        loop(0, per, ship)

    loop(0, 4, project)
    p_own().wait()
    loop(1, SHARDS, lambda i: p_arrival(ahead(m, i, SHARDS)).wait_recv())

    square = jnp.zeros((owned, 1), jnp.float32)
    for c in range(QUARTERS):
        cols = slice(c * WIDTH, (c + 1) * WIDTH)
        value = hidden[:, cols].astype(jnp.float32)
        for head in range(KVH):
            value = value + got[QUARTERS * head + c].astype(jnp.float32)
        mixed[:, cols] = value
        residual[:, cols] = value.astype(jnp.bfloat16)
        square = square + jnp.sum(value * value, axis=-1, keepdims=True)
    factor = lax.rsqrt(square / D + eps_norm)
    normed[...] = (mixed[...] * factor * gain[...].astype(jnp.float32)).astype(jnp.bfloat16)

    for i in range(1, QUARTERS):
        part_copy(i).wait_send()
        lse_copy(i).wait_send()
        g_copy(i).wait_send()
    loop(1, SHARDS, lambda i: p_copy(ahead(m, i, SHARDS)).wait_send())


def merge(part, lse, w, hidden, gain):
    bf, f32 = jnp.bfloat16, jnp.float32
    dma = pltpu.SemaphoreType.DMA
    owned = REQ * QMAX // SHARDS
    return pl.pallas_call(
        merge_kernel,
        out_shape=(jax.ShapeDtypeStruct((owned, D), bf), jax.ShapeDtypeStruct((owned, D), bf)),
        in_specs=[VMEM, VMEM, ANY, VMEM, VMEM],
        out_specs=(VMEM, VMEM),
        scratch_shapes=[
            pltpu.VMEM((QUARTERS, D // SHARDS, WIDTH), bf),
            pltpu.VMEM((QUARTERS, HD, ROWS), bf),
            pltpu.VMEM((QUARTERS, 8, ROWS), f32),
            pltpu.VMEM((ROWS, HD), f32),
            pltpu.VMEM((REQ, QMAX, GROUP * HD), bf),
            pltpu.VMEM((REQ * QMAX, WIDTH), bf),
            pltpu.VMEM((SHARDS, owned, WIDTH), bf),
            pltpu.VMEM((owned, D), f32),
            dma, dma,
            dma((QUARTERS,)), dma((QUARTERS,)),
            dma((QUARTERS,)), dma((QUARTERS,)),
            dma((QUARTERS,)), dma((QUARTERS,)),
            dma((SHARDS,)), dma((SHARDS,)),
        ],
        compiler_params=pltpu.CompilerParams(
            collective_id=1, has_side_effects=True, vmem_limit_bytes=48 << 20
        ),
        name="merge",
    )(part, lse, w, hidden, gain)


def on_device(
    kv_store, retrieval, positions, lengths, queries, new_kv, hidden, out_weight, norm_gain
):
    z = lax.axis_index("store")
    m = lax.axis_index("mp")
    tokens = queries.shape[1]
    context = R * CTOK
    own_places = (context + m * tokens + jnp.arange(tokens, dtype=jnp.int32)).astype(jnp.float32)
    cos_own, sin_own = turns(own_places)
    q = rotate(
        queries.reshape(REQ, tokens, HEADS, HD).astype(jnp.float32),
        cos_own[None, :, None], sin_own[None, :, None],
    ).astype(jnp.bfloat16)
    q = jnp.transpose(q.reshape(REQ, tokens, KVH, GROUP, HD), (2, 0, 1, 3, 4))
    q = q.reshape(KVH, REQ, tokens * GROUP, HD)
    pair = new_kv.reshape(REQ, tokens, KVH, 2, HD)
    own_keys = rotate(
        pair[:, :, :, 0].astype(jnp.float32), cos_own[None, :, None], sin_own[None, :, None]
    ).astype(jnp.bfloat16)
    fresh = jnp.stack([own_keys, pair[:, :, :, 1]], axis=3).reshape(REQ * tokens, KVH * 2 * HD)

    kv_all, q_all, fresh_all, w_all = spread(kv_store, q, fresh, out_weight)

    ids = lax.dynamic_slice_in_dim(retrieval, z * REQ, REQ, 0).reshape(-1)
    cos_at, sin_at = turns((jnp.arange(R, dtype=jnp.int32) * CTOK).astype(jnp.float32))
    part, lse = attend(
        ids, positions.reshape(-1), lengths, q_all.reshape(REQ, ROWS, HD),
        fresh_all.reshape(KVH * 16, 2 * HD), cos_at, sin_at,
        kv_all.reshape(STORES * HELD, CTOK // QUARTERS, 2 * HD),
    )
    residual, normed = merge(part, lse, w_all, hidden.reshape(REQ * tokens, D), norm_gain.reshape(1, D))
    return residual.reshape(REQ, tokens, D), normed.reshape(REQ, tokens, D)


def solution(mesh):
    return jax.shard_map(
        on_device,
        mesh=mesh,
        in_specs=(
            P("store", "mp", None),
            P(),
            P("store", None),
            P("store"),
            P("store", "mp", None),
            P("store", "mp", None),
            P("store", "mp", None),
            P("mp", None),
            P(),
        ),
        out_specs=(P("store", "mp", None), P("store", "mp", None)),
        check_vma=False,
    )
```

time: 506 us -> 193 us (0.38)
  waiting for transfers between devices: 344 us -> 0 us
  Pallas kernels: 0 us -> 177 us
  other arithmetic: 57.5 us -> 1.65 us
  local copies, waits for them, and re-layouts: 48.2 us -> 13 us
  starting transfers between devices: 21.3 us -> 0 us
  matrix products: 19.3 us -> 0 us
  between operations: 15 us -> 0.81 us
    pallas_call x0 -> x3, Pallas kernels: none -> 177 us  [the longest x1 98.4 us: spread(): pl.pallas_call(spread_kernel, out_shape=(jax.ShapeDtypeStruct((STORES, HE...]
    unnamed x3 -> x0, waiting for transfers between devices: 145 us -> none
    all_to_all x3 -> x0, waiting for transfers between devices: 113 us -> none  [the longest x1 105 us: on_device(): lax.all_to_all(stretch_send, 'mp', split_axis=2, concat_axis=1, tiled=True)]
    all_gather x1 -> x0, waiting for transfers between devices: 86 us -> none  [on_device(): block_rows = lax.all_gather(kv_store, 'store', axis=0, tiled=True)]
    sub x1 -> x0, other arithmetic: 24.1 us -> none  [on_device(): exponent = jnp.where(allowed[None, None], jnp.exp(scores - highest), 0.0)]
    all_to_all x3 -> x0, starting transfers between devices: 21 us -> none  [the longest x1 8.59 us: on_device(): lax.all_to_all(fresh_send, 'mp', split_axis=2, concat_axis=1, tiled=True)]
    dot_general x3 -> x0, matrix products: 19.3 us -> none  [the longest x1 10 us: on_device(): jnp.einsum('bthd,bsd->bhts', query_head, all_keys, preferred_element_type...]
    slice x1 -> x0, other arithmetic: 17.4 us -> none  [on_device(): stretch_values = stretch_head[:, :, :, 1].reshape(req_here, -1, head_dim)]
  transfers between devices with their start and end apart: 5 -> 0, of which waited for: 4 -> 0; matrix products, arithmetic and copies ran while one was open for 3% -> 0% of each run, Pallas kernels for 0% -> 0%
where the time goes in v1:
time: 193 us; the launch traced here: 192 us
  Pallas kernels  177 us (92%)
  local copies, waits for them, and re-layouts  13 us (7%)
    pallas_call x1, Pallas kernels, spread(): pl.pallas_call(spread_kernel, out_shape=(jax.ShapeDtypeStruct((STORES, HE...  98.4 us
    pallas_call x1, Pallas kernels, merge(): pl.pallas_call(merge_kernel, out_shape=(jax.ShapeDtypeStruct((owned, D),...  62.6 us
    pallas_call x1, Pallas kernels, attend(): pl.pallas_call(attend_kernel, out_shape=(jax.ShapeDtypeStruct((REQ, HD, R...  15.7 us
    unnamed x20, local copies, waits for them, and re-layouts  7.67 us

profile of v1, /device:TPU:1, one launch (start us, length us, event | category | flops | bytes accessed | tf_op | source)
XLA Modules:
  0.0 192.2 jit_solution(7557489465280699853)
XLA Ops:
  0.6 0.0 copy-start
  0.6 0.0 copy-start.6
  0.7 0.1 multiply_cosine_fusion.1
  0.8 0.1 pad_maximum_fusion.3
  0.9 0.9 reshape.102
  1.8 0.1 slice_convert_fusion
  1.9 0.1 slice_bitcast_fusion.3
  2.0 0.1 fusion.4
  2.1 0.1 copy.18
  2.1 0.1 pad_maximum_fusion
  2.3 0.7 reshape.103.fresh
  2.9 1.2 reshape.112
  4.1 0.2 slice_bitcast_fusion.1
  4.3 0.0 copy-start.9
  4.3 0.0 copy-start.5
  4.4 0.0 copy-done.6
  4.4 0.2 reshape.111
  4.6 0.9 copy_bitcast_fusion.q
  5.5 98.4 %spread.1 = (bf16[8,16,128,256]{3,2,1,0:T(8,128)(2,1)}, bf16[4,32,32,128]{3,2,1,0:T(8,128)(2,1)}, bf16[8,16,256]{2,1,0:T(8,128)(2,1)}, bf16[4,256,2048]{2,1,0:T(8,128)(2,1)}) custom-call(bf16[16,16,2048]{2,1,0:T(8,128)(2,1)} %kv.1, bf16[8,4,32,128]{3,2,1,0:T(8,128)(2,1)} %copy_bitcast_fusion.q, bf16[16,2048]{1,0:T(8,128)(2,1)} %reshape.103.fresh, ...), custom_call_target="tpu_custom_call" | custom-call | tf_op jit(solution)/shard_map/spread/pallas_call | solution.py:222
  104.0 0.1 fusion.5
  104.1 0.1 pad_maximum_fusion.1
  104.2 0.0 copy-done
  104.2 0.1 constant_dynamic-slice_fusion
  104.3 0.1 copy.15
  104.3 0.1 reshape.99.ids
  104.4 0.0 copy-done.9
  104.4 0.1 reshape.100.places
  104.5 0.0 copy-done.5
  104.5 0.0 copy-start.1
  104.5 3.4 %copy-done.1 = bf16[8,16,128,256]{3,2,1,0:T(8,128)(2,1)S(1)} copy-done((bf16[8,16,128,256]{3,2,1,0:T(8,128)(2,1)S(1)}, bf16[8,16,128,256]{3,2,1,0:T(8,128)(2,1)}, u32[]{:S(2)}) %copy-start.1) | copy-done | bytes 8388632
  107.9 0.0 copy-start.3
  107.9 1.2 copy-done.3
  109.1 0.0 copy-start.4
  109.1 0.8 copy-done.4
  110.0 0.0 copy-start.7
  110.0 0.0 copy-start.8
  110.0 15.7 %attend.1 = (bf16[4,128,1024]{2,1,0:T(8,128)(2,1)S(1)}, f32[4,8,1024]{2,1,0:T(8,128)S(1)}) custom-call(s32[32]{0:T(128)S(1)} %reshape.99.ids, s32[32]{0:T(128)S(1)} %reshape.100.places, s32[4]{0:T(128)S(1)} %copy-done.5, bf16[4,1024,128]{2,1,0:T(8,128)(2,1)S(1)} %bitcast.19, bf16[128,256]{1,0:T(8,128)(2,1)S(1)} %bitcast.20, ...), custom_call_target="tpu_custom_call" | custom-call | tf_op jit(solution)/shard_map/attend/pallas_call | solution.py:310
  125.7 0.0 copy-done.7
  125.7 0.1 reshape.107.hidden
  125.8 0.0 copy-done.8
  125.8 0.0 copy-start.2
  125.8 2.2 %copy-done.2 = bf16[4,256,2048]{2,1,0:T(8,128)(2,1)S(1)} copy-done((bf16[4,256,2048]{2,1,0:T(8,128)(2,1)S(1)}, bf16[4,256,2048]{2,1,0:T(8,128)(2,1)}, u32[]{:S(2)}) %copy-start.2) | copy-done | bytes 4194328
  128.0 62.6 %merge.1 = (bf16[16,8192]{1,0:T(8,128)(2,1)S(1)}, bf16[16,8192]{1,0:T(8,128)(2,1)S(1)}) custom-call(bf16[4,128,1024]{2,1,0:T(8,128)(2,1)S(1)} %get-tuple-element.13.part, f32[4,8,1024]{2,1,0:T(8,128)S(1)} %get-tuple-element.14.lse, bf16[4,256,2048]{2,1,0:T(8,128)(2,1)S(1)} %copy-done.2, bf16[16,8192]{1,0:T(8,128)(2,1)S(1)} %reshape.107.hidden, ...), custom_call_target="tpu_custom_call" | custom-call | tf_op jit(solution)/shard_map/merge/pallas_call | solution.py:474
  190.6 0.8 reshape.109
  191.4 0.8 reshape.110
  (4 shorter events, 0.0 us)
Async XLA Ops:
  0.6 103.6 %copy-start = (s32[32,8]{0,1:T(8,128)S(1)}, s32[32,8]{0,1:T(8,128)}, u32[]{:S(2)}) copy-start(s32[32,8]{0,1:T(8,128)} %param.10) | copy-start | bytes 3076
  0.6 3.7 %copy-start.6 = (bf16[4,4,8192]{2,1,0:T(4,128)(2,1)S(1)}, bf16[4,4,8192]{2,1,0:T(4,128)(2,1)}, u32[]{:S(2)}) copy-start(bf16[4,4,8192]{2,1,0:T(4,128)(2,1)} %param.13) | copy-start | bytes 786436
  4.3 100.1 %copy-start.9 = (s32[4,8]{1,0:T(4,128)S(1)}, s32[4,8]{1,0:T(4,128)}, u32[]{:S(2)}) copy-start(s32[4,8]{1,0:T(4,128)} %param.11) | copy-start | bytes 388
  4.3 100.2 %copy-start.5 = (s32[4]{0:T(128)S(1)}, s32[4]{0:T(128)}, u32[]{:S(2)}) copy-start(s32[4]{0:T(128)} %lengths.1) | copy-start | bytes 52
  104.5 3.4 %copy-start.1 = (bf16[8,16,128,256]{3,2,1,0:T(8,128)(2,1)S(1)}, bf16[8,16,128,256]{3,2,1,0:T(8,128)(2,1)}, u32[]{:S(2)}) copy-start(bf16[8,16,128,256]{3,2,1,0:T(8,128)(2,1)} %get-tuple-element.12) | copy-start | bytes 25165828
  107.9 1.2 copy-start.3
  109.1 0.8 copy-start.4
  110.0 15.7 %copy-start.7 = (bf16[4,4,8192]{2,1,0:T(4,128)(2,1)S(1)}, bf16[4,4,8192]{2,1,0:T(4,128)(2,1)}, u32[]{:S(2)}) copy-start(bf16[4,4,8192]{2,1,0:T(4,128)(2,1)} %param.15) | copy-start | bytes 786436
  110.0 15.8 %copy-start.8 = (bf16[8192]{0:T(1024)(128)(2,1)S(1)}, bf16[8192]{0:T(1024)(128)(2,1)}, u32[]{:S(2)}) copy-start(bf16[8192]{0:T(1024)(128)(2,1)} %param.17) | copy-start | bytes 49156
  125.8 2.2 %copy-start.2 = (bf16[4,256,2048]{2,1,0:T(8,128)(2,1)S(1)}, bf16[4,256,2048]{2,1,0:T(8,128)(2,1)}, u32[]{:S(2)}) copy-start(bf16[4,256,2048]{2,1,0:T(8,128)(2,1)} %get-tuple-element.15.w_hbm) | copy-start | bytes 12582916

commit v2 on v1

v2 whole, which is shorter than its diff:
```python
import jax
import jax.numpy as jnp
import numpy as np
from jax import lax
from jax.experimental import pallas as pl
from jax.experimental.pallas import tpu as pltpu
from jax.sharding import PartitionSpec as P

MESH = pl.DeviceIdType.MESH
HBM = pl.BlockSpec(memory_space=pltpu.HBM)
VMEM = pl.BlockSpec(memory_space=pltpu.VMEM)
SMEM = pl.BlockSpec(memory_space=pltpu.SMEM)

STORES = 8
SHARDS = 32
HEADS = 64
KVH = 8
GROUP = 8
HD = 128
D = 8192
QUARTERS = 4
CTOK = 512
R = 8
REQ = 4
QMAX = 128
HELD = 16
CHUNKS = 4
PER = HELD // CHUNKS
RING = 8
WIDTH = D // RING
ROWS = QMAX * GROUP
BLOCK = 512
TOKENS = QMAX // SHARDS
OWNED = REQ * TOKENS
LOG2E = 1.4426950408889634

theta_base = 1000000.0
eps_norm = 1e-06


def turns(places):
    inv_freq = np.float32(theta_base) ** (-(np.arange(HD // 2, dtype=np.float32) * np.float32(2.0)) / np.float32(HD))
    angles = np.asarray(places, np.float32)[..., None] * inv_freq
    cosines, sines = np.cos(angles), np.sin(angles)
    return (
        jnp.asarray(np.concatenate([cosines, cosines], axis=-1)),
        jnp.asarray(np.concatenate([-sines, sines], axis=-1)),
    )


def rotate(field_in, cosines, sines):
    return field_in * cosines + pltpu.roll(field_in, HD // 2, 1) * sines


def ahead(a, b, n):
    return lax.rem(a + b, n)


def spread_kernel(
    kv, queries, new_kv, cosines, sines, w, kv_all, q_all, fresh_all, w_all,
    q_wide, q, fresh_wide, fresh, own_sem, kv_send, kv_recv, q_send, q_recv, f_send, f_recv, w_send, w_recv, z_send, z_recv,
):
    m = lax.axis_index("mp")
    z = lax.axis_index("store")
    k = m // QUARTERS
    j = lax.rem(m, QUARTERS)
    right, left = ahead(z, 1, STORES), ahead(z, STORES - 1, STORES)

    barrier = pltpu.get_barrier_semaphore()

    def greet(i, carry):
        pl.semaphore_signal(barrier, 1, device_id={"mp": ahead(m, i, SHARDS)}, device_id_type=MESH)
        return carry

    lax.fori_loop(1, SHARDS, greet, 0)
    for near in (left, right):
        pl.semaphore_signal(barrier, 1, device_id={"store": near}, device_id_type=MESH)
    pl.semaphore_wait(barrier, SHARDS + 1)

    def remote(src, dst, send, recv, **where):
        return pltpu.make_async_remote_copy(
            src_ref=src, dst_ref=dst, send_sem=send, recv_sem=recv, device_id=where, device_id_type=MESH
        )

    def kv_rows(c, head):
        return kv_all.at[z, pl.ds(PER * c, PER), pl.ds(pl.multiple_of(16 * head, 16), 16), :]

    def kv_part(c, head):
        return kv.at[pl.ds(PER * c, PER), :, pl.ds(pl.multiple_of(2 * HD * head, 2 * HD), 2 * HD)]

    def kv_copy(c, i):
        to = ahead(k, i, KVH)
        return remote(
            kv_part(c, to), kv_rows(c, k), kv_send.at[c, i], kv_recv.at[c, k], mp=QUARTERS * to + j
        )

    def kv_arrival(c, i):
        come = ahead(k, i, KVH)
        return remote(
            kv_part(c, come), kv_rows(c, come), kv_send.at[c, i], kv_recv.at[c, come], mp=QUARTERS * come + j
        )

    def own_kv(c):
        return pltpu.make_async_copy(kv_part(c, k), kv_rows(c, k), own_sem.at[c])

    for c in range(CHUNKS):
        own_kv(c).start()

        def send_kv(i, carry):
            kv_copy(c, i).start()
            return carry

        lax.fori_loop(1, KVH, send_kv, 0)

    def z_copy(way, s, c):
        owner = ahead(z, (STORES - s) if way == 0 else s, STORES)
        slab = kv_all.at[owner, pl.ds(PER * c, PER)]
        return remote(
            slab, slab, z_send.at[way, s, c], z_recv.at[way, s, c], store=right if way == 0 else left
        )

    def z_arrival(way, s, c):
        owner = ahead(z, (STORES - 1 - s) if way == 0 else (s + 1), STORES)
        slab = kv_all.at[owner, pl.ds(PER * c, PER)]
        return remote(
            slab, slab, z_send.at[way, s, c], z_recv.at[way, s, c], store=right if way == 0 else left
        )

    for c in range(CHUNKS):
        own_kv(c).wait()

        def take_kv(i, carry):
            kv_arrival(c, i).wait_recv()
            return carry

        lax.fori_loop(1, KVH, take_kv, 0)
        for way in range(2):
            z_copy(way, 0, c).start()

    def fresh_part(head):
        return fresh.at[:, pl.ds(pl.multiple_of(2 * HD * head, 2 * HD), 2 * HD)]

    def f_copy(i):
        to = ahead(k, i, KVH)
        return remote(fresh_part(to), fresh_all.at[k], f_send.at[i], f_recv.at[k], mp=QUARTERS * to + j)

    def f_arrival(i):
        come = ahead(k, i, KVH)
        return remote(fresh_part(come), fresh_all.at[come], f_send.at[i], f_recv.at[come], mp=QUARTERS * come + j)

    def q_copy(i):
        to = ahead(m, i, SHARDS)
        return remote(q.at[to // QUARTERS], q_all.at[:, m], q_send.at[i], q_recv.at[m], mp=to)

    def q_arrival(i):
        come = ahead(m, i, SHARDS)
        return remote(q.at[k], q_all.at[:, come], q_send.at[i], q_recv.at[come], mp=come)

    ring = RING * (m // RING)
    place = lax.rem(m, RING)

    def w_part(block):
        return w.at[:, pl.ds(pl.multiple_of(WIDTH * block, WIDTH), WIDTH)]

    def w_copy(i):
        to = ahead(place, i, RING)
        return remote(w_part(to), w_all.at[place], w_send.at[i], w_recv.at[place], mp=ring + to)

    def w_arrival(i):
        come = ahead(place, i, RING)
        return remote(w_part(come), w_all.at[come], w_send.at[i], w_recv.at[come], mp=ring + come)

    own = [
        pltpu.make_async_copy(fresh_part(k), fresh_all.at[k], own_sem.at[CHUNKS]),
        pltpu.make_async_copy(q.at[k], q_all.at[:, m], own_sem.at[CHUNKS + 1]),
    ]

    def loop(low, high, act):
        def body(i, carry):
            act(i)
            return carry

        lax.fori_loop(low, high, body, 0)

    loop(1, RING, lambda i: w_copy(i).start())

    cos, sin = cosines[m], sines[m]

    def turn(head):
        for b in range(REQ):
            for g in range(GROUP):
                at = pl.ds(pl.multiple_of((head * GROUP + g) * HD, HD), HD)
                value = rotate(queries[b, :, at].astype(jnp.float32), cos, sin)
                q_wide[head, b, pl.ds(g, TOKENS, stride=GROUP), :] = value
            at = pl.multiple_of(2 * HD * head, 2 * HD)
            key = rotate(new_kv[b, :, pl.ds(at, HD)].astype(jnp.float32), cos, sin)
            fresh_wide[b * TOKENS : (b + 1) * TOKENS, pl.ds(at, HD)] = key
            at = pl.multiple_of(at + HD, HD)
            fresh_wide[b * TOKENS : (b + 1) * TOKENS, pl.ds(at, HD)] = new_kv[b, :, pl.ds(at, HD)].astype(jnp.float32)
        q[head] = q_wide[head].astype(jnp.bfloat16)

    loop(0, KVH, turn)
    fresh[...] = fresh_wide[...].astype(jnp.bfloat16)
    for copy in own:
        copy.start()
    loop(1, KVH, lambda i: f_copy(i).start())
    loop(1, SHARDS, lambda i: q_copy(i).start())

    last = STORES // 2 - 1
    halves = (range(CHUNKS // 2), range(CHUNKS // 2, CHUNKS))
    for s in range(1, last + 1):
        for c in range(CHUNKS):
            for way in range(2):
                if s < last or c in halves[way]:
                    z_arrival(way, s - 1, c).wait_recv()
                    z_copy(way, s, c).start()
    for way in range(2):
        for c in range(CHUNKS):
            if c in halves[way]:
                z_arrival(way, last, c).wait_recv()
            else:
                z_arrival(way, last - 1, c).wait_recv()

    for copy in own:
        copy.wait()
    loop(1, RING, lambda i: w_arrival(i).wait_recv())
    loop(1, KVH, lambda i: f_arrival(i).wait_recv())
    loop(1, SHARDS, lambda i: q_arrival(i).wait_recv())
    loop(1, RING, lambda i: w_copy(i).wait_send())
    loop(1, KVH, lambda i: f_copy(i).wait_send())
    loop(1, SHARDS, lambda i: q_copy(i).wait_send())
    for c in range(CHUNKS):
        loop(1, KVH, lambda i: kv_copy(c, i).wait_send())
    for way in range(2):
        for s in range(last + 1):
            for c in range(CHUNKS):
                if s < last or c in halves[way]:
                    z_copy(way, s, c).wait_send()


def spread(kv, queries, new_kv, cosines, sines, w):
    bf, f32 = jnp.bfloat16, jnp.float32
    dma = pltpu.SemaphoreType.DMA
    return pl.pallas_call(
        spread_kernel,
        out_shape=(
            jax.ShapeDtypeStruct((STORES, HELD, CTOK // QUARTERS, 2 * HD), bf),
            jax.ShapeDtypeStruct((REQ, SHARDS, QMAX // SHARDS * GROUP, HD), bf),
            jax.ShapeDtypeStruct((KVH, 16, 2 * HD), bf),
            jax.ShapeDtypeStruct((RING, D // SHARDS, WIDTH), bf),
        ),
        in_specs=[HBM] + [VMEM] * 4 + [HBM],
        out_specs=(HBM,) * 4,
        scratch_shapes=[
            pltpu.VMEM((KVH, REQ, TOKENS * GROUP, HD), f32),
            pltpu.VMEM((KVH, REQ, TOKENS * GROUP, HD), bf),
            pltpu.VMEM((OWNED, KVH * 2 * HD), f32),
            pltpu.VMEM((OWNED, KVH * 2 * HD), bf),
            dma((CHUNKS + 2,)),
            dma((CHUNKS, KVH)), dma((CHUNKS, KVH)),
            dma((SHARDS,)), dma((SHARDS,)),
            dma((KVH,)), dma((KVH,)),
            dma((RING,)), dma((RING,)),
            dma((2, STORES // 2, CHUNKS)), dma((2, STORES // 2, CHUNKS)),
        ],
        compiler_params=pltpu.CompilerParams(
            collective_id=0, has_side_effects=True, vmem_limit_bytes=60 << 20
        ),
        name="spread",
    )(kv, queries, new_kv, cosines, sines, w)


def attend_kernel(
    retrieval, places, lengths, cosines, sines, q_all, fresh_all, kv_all, out, lse,
    slots, keys, q, fresh, sem, q_sem, fresh_sem,
):
    quarter = CTOK // QUARTERS
    held = R * quarter
    j = lax.rem(lax.axis_index("mp"), QUARTERS)
    z = lax.axis_index("store")

    def fetch(b, r):
        return pltpu.make_async_copy(
            kv_all.at[retrieval[z * REQ + b, r]], slots.at[b, pl.ds(r * quarter, quarter)], sem.at[b, r]
        )

    def fetch_q(b):
        return pltpu.make_async_copy(q_all.at[b], q.at[b], q_sem.at[b])

    fetch_fresh = pltpu.make_async_copy(fresh_all, fresh, fresh_sem)
    for b in range(REQ):
        for r in range(R):
            fetch(b, r).start()
        fetch_q(b).start()
        if b == 0:
            fetch_fresh.start()
    fetch_fresh.wait()
    for b in range(REQ):
        slots[b, held:, :] = fresh[...]
    keys[held:, :] = fresh[:, :HD]
    col = lax.broadcasted_iota(jnp.int32, (BLOCK, quarter), 1)
    fresh_token = TOKENS * (QUARTERS * (col >> 4) + j) + (col & 3)
    fresh_request = (col >> 2) & 3
    row = lax.broadcasted_iota(jnp.int32, (BLOCK, quarter), 0)
    for b in range(REQ):
        for r in range(R):
            fetch(b, r).wait()
        for r in range(R):
            at = places[b, r]
            key = slots[b, r * quarter : (r + 1) * quarter, :HD].astype(jnp.float32)
            key = rotate(key, cosines[pl.ds(at, 1), :], sines[pl.ds(at, 1), :])
            keys[r * quarter : (r + 1) * quarter, :] = key.astype(jnp.bfloat16)
        fetch_q(b).wait()
        length = lengths[b]

        def block(i, carry):
            span = pl.ds(pl.multiple_of(i * BLOCK, BLOCK), BLOCK)
            scores = lax.dot_general(
                q[b, span, :], keys[...], (((1,), (1,)), ((), ())), preferred_element_type=jnp.float32
            ) * (HD**-0.5 * LOG2E)
            allowed = (fresh_request == b) & (fresh_token <= ((i * BLOCK + row) >> 3))
            fresh_scores = jnp.where(allowed, scores[:, held:], -1e30)
            scores = scores[:, :held]
            top = jnp.maximum(
                jnp.max(scores, axis=1, keepdims=True), jnp.max(fresh_scores, axis=1, keepdims=True)
            )
            expo, fresh_expo = jnp.exp2(scores - top), jnp.exp2(fresh_scores - top)
            total = jnp.sum(expo, axis=1, keepdims=True) + jnp.sum(fresh_expo, axis=1, keepdims=True)
            sums = jnp.dot(
                expo.astype(jnp.bfloat16), slots[b, :held, HD:], preferred_element_type=jnp.float32
            ) + jnp.dot(
                fresh_expo.astype(jnp.bfloat16), slots[b, held:, HD:], preferred_element_type=jnp.float32
            )
            out[b, span, :] = jnp.where(i * BLOCK + row < length * GROUP, sums / total, 0.0).astype(jnp.bfloat16)
            logs = top + jnp.log(total) * LOG2E
            lse[b, :, span] = jnp.broadcast_to(logs, (BLOCK, HD)).T[:8]
            return carry

        def blank(i, carry):
            span = pl.ds(pl.multiple_of(i * BLOCK, BLOCK), BLOCK)
            out[b, span, :] = jnp.zeros((BLOCK, HD), jnp.bfloat16)
            lse[b, :, span] = jnp.zeros((8, BLOCK), jnp.float32)
            return carry

        used = (length * GROUP + BLOCK - 1) // BLOCK
        lax.fori_loop(0, used, block, 0)
        lax.fori_loop(used, ROWS // BLOCK, blank, 0)


def attend(retrieval, places, lengths, cosines, sines, q_all, fresh_all, kv_all):
    quarter = CTOK // QUARTERS
    bf = jnp.bfloat16
    dma = pltpu.SemaphoreType.DMA
    return pl.pallas_call(
        attend_kernel,
        out_shape=(
            jax.ShapeDtypeStruct((REQ, ROWS, HD), bf),
            jax.ShapeDtypeStruct((REQ, 8, ROWS), jnp.float32),
        ),
        in_specs=[SMEM] * 3 + [VMEM] * 2 + [HBM] * 3,
        out_specs=(VMEM, VMEM),
        scratch_shapes=[
            pltpu.VMEM((REQ, (R + 1) * quarter, 2 * HD), bf),
            pltpu.VMEM(((R + 1) * quarter, HD), bf),
            pltpu.VMEM((REQ, ROWS, HD), bf),
            pltpu.VMEM((quarter, 2 * HD), bf),
            dma((REQ, R)), dma((REQ,)), dma,
        ],
        compiler_params=pltpu.CompilerParams(vmem_limit_bytes=60 << 20),
        name="attend",
    )(retrieval, places, lengths, cosines, sines, q_all, fresh_all, kv_all)


def merge_kernel(
    part, lse, w_own, w_all, hidden, gain, residual, normed,
    w, from_mate, from_mate_lse, pair, pair_lse, from_chip, from_chip_lse, rows, attended, sent, got, mixed,
    w_sem, own_sem, c_send, c_recv, l_send, l_recv, g_send, g_recv, p_send, p_recv,
):
    m = lax.axis_index("mp")
    k = m // QUARTERS
    j = lax.rem(m, QUARTERS)
    core, half = lax.rem(j, 2), j // 2
    mate, chip = m + 1 - 2 * core, QUARTERS * k + ahead(j, 2, QUARTERS)
    ring = RING * (m // RING)
    place = lax.rem(m, RING)
    w_loads = [
        pltpu.make_async_copy(
            w_own.at[:, pl.ds(pl.multiple_of(WIDTH * place, WIDTH), WIDTH)], w.at[place], w_sem.at[0]
        )
    ]
    for i in range(1, RING):
        come = ahead(place, i, RING)
        w_loads.append(pltpu.make_async_copy(w_all.at[come], w.at[come], w_sem.at[i]))
    for load in w_loads:
        load.start()

    barrier = pltpu.get_barrier_semaphore()

    def loop(low, high, act):
        def body(i, carry):
            act(i)
            return carry

        lax.fori_loop(low, high, body, 0)

    loop(
        1,
        SHARDS,
        lambda i: pl.semaphore_signal(
            barrier, 1, device_id={"mp": ahead(m, i, SHARDS)}, device_id_type=MESH
        ),
    )
    pl.semaphore_wait(barrier, SHARDS - 1)

    def remote(src, dst, send, recv, to):
        return pltpu.make_async_remote_copy(
            src_ref=src, dst_ref=dst, send_sem=send, recv_sem=recv, device_id={"mp": to}, device_id_type=MESH
        )

    def mate_copies(at, n):
        give = 1 - core + 2 * at
        return (
            remote(lse.at[give], from_mate_lse.at[at], l_send.at[n], l_recv.at[n], mate),
            remote(part.at[give], from_mate.at[at], c_send.at[n], c_recv.at[n], mate),
        )

    def combine(one, one_log, two, two_log):
        top = jnp.maximum(one_log, two_log)
        one_share, two_share = jnp.exp2(one_log - top), jnp.exp2(two_log - top)
        total = one_share + two_share
        share = jnp.broadcast_to(one_share / total, (HD, ROWS)).T
        return two + (one - two) * share, top + jnp.log(total) * LOG2E

    def wide(ref, at):
        return ref[at].astype(jnp.float32)

    pair_copies = (
        remote(pair_lse, from_chip_lse, l_send.at[2], l_recv.at[2], chip),
        remote(pair, from_chip, c_send.at[2], c_recv.at[2], chip),
    )
    other = 1 - half
    order = ((other, 0), (half, 1))
    for at, n in order:
        for copy in mate_copies(at, n):
            copy.start()
    for copy in mate_copies(other, 0):
        copy.wait_recv()
    give = core + 2 * other
    value, logs = combine(
        wide(part, give), lse[give, :1, :], wide(from_mate, other), from_mate_lse[other, :1, :]
    )
    pair[...] = value.astype(jnp.bfloat16)
    pair_lse[...] = jnp.broadcast_to(logs, (8, ROWS))
    for copy in pair_copies:
        copy.start()
    for copy in mate_copies(half, 1):
        copy.wait_recv()
    value, logs = combine(
        wide(part, j), lse[j, :1, :], wide(from_mate, half), from_mate_lse[half, :1, :]
    )
    rows[...] = value
    for copy in pair_copies:
        copy.wait_recv()
    value, logs = combine(rows[...], logs, from_chip[...].astype(jnp.float32), from_chip_lse[:1, :])
    rows[...] = value
    for h in range(GROUP):
        attended[place, :, h * HD : (h + 1) * HD] = rows[pl.ds(h, QMAX, stride=GROUP), :].astype(jnp.bfloat16)

    def g_copy(at, n, to):
        return remote(attended.at[at], attended.at[at], g_send.at[n], g_recv.at[n], to)

    hops = (2, 6, 4)
    mate_place = place + 1 - 2 * core
    g_copy(place, 0, mate).start()
    for n, hop in enumerate(hops):
        g_copy(place, 1 + n, ring + ahead(place, hop, RING)).start()
    for load in w_loads:
        load.wait()
    for n, hop in enumerate(hops):
        come = ahead(place, RING - hop, RING)
        g_copy(come, 1 + n, mate).wait_recv()
        g_copy(come, 4 + n, mate).start()
    g_copy(mate_place, 0, mate).wait_recv()
    for n, hop in enumerate(hops):
        g_copy(ahead(mate_place, RING - hop, RING), 4 + n, mate).wait_recv()

    owned = OWNED
    span = REQ * QMAX // 4
    per = span // owned

    def p_copy(to):
        return remote(
            sent.at[pl.ds(pl.multiple_of(owned * to, owned), owned), :], got.at[m], p_send.at[to], p_recv.at[m], to
        )

    def p_own():
        return pltpu.make_async_copy(
            sent.at[pl.ds(pl.multiple_of(owned * m, owned), owned), :], got.at[m], own_sem
        )

    def p_arrival(come):
        return remote(
            sent.at[pl.ds(pl.multiple_of(owned * come, owned), owned), :], got.at[come], p_send.at[come], p_recv.at[come], come
        )

    def project(i):
        block = ahead(m // per, i, 4)
        at = block * span + lax.broadcasted_iota(jnp.int32, (span, REQ * QMAX), 0)
        source = QMAX * ((at >> 2) & 3) + 4 * (at >> 4) + (at & 3)
        pick = (source == lax.broadcasted_iota(jnp.int32, (span, REQ * QMAX), 1)).astype(jnp.bfloat16)
        total = None
        for g in range(RING // REQ):
            chosen = jnp.dot(
                pick,
                attended[REQ * g : REQ * (g + 1)].reshape(REQ * QMAX, GROUP * HD),
                preferred_element_type=jnp.float32,
            ).astype(jnp.bfloat16)
            term = jnp.dot(
                chosen,
                w[REQ * g : REQ * (g + 1)].reshape(GROUP * HD, WIDTH),
                preferred_element_type=jnp.float32,
            )
            total = term if total is None else total + term
        sent[pl.ds(pl.multiple_of(block * span, span), span), :] = total.astype(jnp.bfloat16)

        def ship(t):
            to = block * per + ahead(m, t, per)

            @pl.when(to != m)
            def _():
                p_copy(to).start()

            @pl.when(to == m)
            def _():
                p_own().start()

        loop(0, per, ship)

    loop(0, 4, project)
    p_own().wait()
    loop(1, SHARDS, lambda i: p_arrival(ahead(m, i, SHARDS)).wait_recv())

    square = jnp.zeros((owned, 1), jnp.float32)
    for c in range(RING):
        cols = slice(c * WIDTH, (c + 1) * WIDTH)
        value = jnp.concatenate([hidden[b, :, cols].astype(jnp.float32) for b in range(REQ)], axis=0)
        for group in range(SHARDS // RING):
            value = value + got[RING * group + c].astype(jnp.float32)
        mixed[:, cols] = value
        square = square + jnp.sum(value * value, axis=-1, keepdims=True)
    factor = lax.rsqrt(square / D + eps_norm)
    for b in range(REQ):
        mine = slice(b * TOKENS, (b + 1) * TOKENS)
        residual[b] = mixed[mine, :].astype(jnp.bfloat16)
        normed[b] = (mixed[mine, :] * factor[mine] * gain[...].astype(jnp.float32)).astype(jnp.bfloat16)

    for at, n in order:
        for copy in mate_copies(at, n):
            copy.wait_send()
    for copy in pair_copies:
        copy.wait_send()
    g_copy(place, 0, mate).wait_send()
    for n, hop in enumerate(hops):
        g_copy(place, 1 + n, mate).wait_send()
        g_copy(ahead(place, RING - hop, RING), 4 + n, mate).wait_send()
    loop(1, SHARDS, lambda i: p_copy(ahead(m, i, SHARDS)).wait_send())


def merge(part, lse, w_own, w_all, hidden, gain):
    bf, f32 = jnp.bfloat16, jnp.float32
    dma = pltpu.SemaphoreType.DMA
    owned = OWNED
    return pl.pallas_call(
        merge_kernel,
        out_shape=(jax.ShapeDtypeStruct((REQ, TOKENS, D), bf),) * 2,
        in_specs=[VMEM, VMEM, HBM, HBM, VMEM, VMEM],
        out_specs=(VMEM, VMEM),
        scratch_shapes=[
            pltpu.VMEM((RING, D // SHARDS, WIDTH), bf),
            pltpu.VMEM((2, ROWS, HD), bf),
            pltpu.VMEM((2, 8, ROWS), f32),
            pltpu.VMEM((ROWS, HD), bf),
            pltpu.VMEM((8, ROWS), f32),
            pltpu.VMEM((ROWS, HD), bf),
            pltpu.VMEM((8, ROWS), f32),
            pltpu.VMEM((ROWS, HD), f32),
            pltpu.VMEM((RING, QMAX, GROUP * HD), bf),
            pltpu.VMEM((REQ * QMAX, WIDTH), bf),
            pltpu.VMEM((SHARDS, owned, WIDTH), bf),
            pltpu.VMEM((owned, D), f32),
            dma((RING,)), dma,
            dma((3,)), dma((3,)),
            dma((3,)), dma((3,)),
            dma((7,)), dma((7,)),
            dma((SHARDS,)), dma((SHARDS,)),
        ],
        compiler_params=pltpu.CompilerParams(
            collective_id=1, has_side_effects=True, vmem_limit_bytes=60 << 20
        ),
        name="merge",
    )(part, lse, w_own, w_all, hidden, gain)


def on_device(
    kv_store, retrieval, positions, lengths, queries, new_kv, hidden, out_weight, norm_gain
):
    context = R * CTOK
    cos_own, sin_own = turns(np.arange(context, context + QMAX))
    shape = (SHARDS, TOKENS, HD)
    kv_all, q_all, fresh_all, w_all = spread(
        kv_store, queries, new_kv, cos_own.reshape(shape), sin_own.reshape(shape), out_weight
    )
    cos_at, sin_at = turns(np.arange(R) * CTOK)
    part, lse = attend(
        retrieval, positions, lengths, cos_at, sin_at, q_all.reshape(REQ, ROWS, HD),
        fresh_all.reshape(KVH * 16, 2 * HD),
        kv_all.reshape(STORES * HELD, CTOK // QUARTERS, 2 * HD),
    )
    return merge(part, lse, out_weight, w_all, hidden, norm_gain.reshape(1, D))


def solution(mesh):
    return jax.shard_map(
        on_device,
        mesh=mesh,
        in_specs=(
            P("store", "mp", None),
            P(),
            P("store", None),
            P("store"),
            P("store", "mp", None),
            P("store", "mp", None),
            P("store", "mp", None),
            P("mp", None),
            P(),
        ),
        out_specs=(P("store", "mp", None), P("store", "mp", None)),
        check_vma=False,
    )
```

time: 193 us -> 173 us (0.90)
  Pallas kernels: 177 us -> 168 us
  local copies, waits for them, and re-layouts: 13 us -> 4.81 us
    pallas_call x2, Pallas kernels: 78.3 us -> 67.8 us  [the longest x1 54.2 us: merge(): pl.pallas_call(merge_kernel, out_shape=(jax.ShapeDtypeStruct((REQ, TOKENS...]
    unnamed x20 -> x7, local copies, waits for them, and re-layouts: 7.67 us -> 4.18 us
    reshape x8 -> x1, local copies, waits for them, and re-layouts: 3.41 us -> 0.63 us  [on_device(): return merge(part, lse, out_weight, w_all, hidden, norm_gain.reshape(1, D))]
where the time goes in v2:
time: 173 us
  Pallas kernels  168 us (97%)
  local copies, waits for them, and re-layouts  4.81 us (3%)
    pallas_call x1, Pallas kernels, spread(): pl.pallas_call(spread_kernel, out_shape=(jax.ShapeDtypeStruct((STORES, HE...  99.7 us
    pallas_call x1, Pallas kernels, merge(): pl.pallas_call(merge_kernel, out_shape=(jax.ShapeDtypeStruct((REQ, TOKENS...  54.2 us
    pallas_call x1, Pallas kernels, attend(): pl.pallas_call(attend_kernel, out_shape=(jax.ShapeDtypeStruct((REQ, ROWS,...  13.6 us
    unnamed x7, local copies, waits for them, and re-layouts  4.18 us

profile of v2, /device:TPU:1, one launch (start us, length us, event | category | flops | bytes accessed | tf_op | source)
XLA Modules:
  0.0 173.1 jit_solution(5943680258271672738)
XLA Ops:
  0.6 0.0 copy-start.1
  0.6 99.7 %spread.1 = (bf16[8,16,128,256]{3,2,1,0:T(8,128)(2,1)}, bf16[4,32,32,128]{3,2,1,0:T(8,128)(2,1)}, bf16[8,16,256]{2,1,0:T(8,128)(2,1)}, bf16[8,256,1024]{2,1,0:T(8,128)(2,1)}) custom-call(bf16[16,16,2048]{2,1,0:T(8,128)(2,1)} %kv.1, bf16[4,4,8192]{2,1,0:T(4,128)(2,1)} %queries.1, bf16[4,4,2048]{2,1,0:T(4,128)(2,1)} %new_kv.1, ...), custom_call_target="tpu_custom_call" | custom-call | tf_op jit(solution)/shard_map/spread/pallas_call | solution.py:244
  100.4 0.0 copy-done.1
  100.4 0.7 copy.15.retrieval
  101.1 0.0 copy-start
  101.1 13.6 %attend.1 = (bf16[4,1024,128]{2,1,0:T(8,128)(2,1)}, f32[4,8,1024]{2,1,0:T(8,128)}) custom-call(s32[32,8]{1,0:T(8,128)} %copy.15.retrieval, s32[4,8]{1,0:T(4,128)} %places.1, s32[4]{0:T(128)} %lengths.1, f32[8,128]{1,0:T(8,128)} %constant.10.clone.cosines, f32[8,128]{1,0:T(8,128)} %constant.11.clone.sines, bf16[4,1024,128]{2,1,0:T(8,128)(2,1)} %bitcast.4, ...), custom_call_target="tpu_custom_call" | custom-call | tf_op jit(solution)/shard_map/attend/pallas_call | solution.py:354
  114.7 0.0 copy-done
  114.7 0.6 reshape.27.gain
  115.4 54.2 %merge.1 = (bf16[4,4,8192]{2,1,0:T(4,128)(2,1)}, bf16[4,4,8192]{2,1,0:T(4,128)(2,1)}) custom-call(bf16[4,1024,128]{2,1,0:T(8,128)(2,1)} %get-tuple-element.11.part, f32[4,8,1024]{2,1,0:T(8,128)} %get-tuple-element.12.lse, bf16[256,8192]{1,0:T(8,128)(2,1)} %w_own.1, bf16[8,256,1024]{2,1,0:T(8,128)(2,1)} %get-tuple-element.13.w_all, ...), custom_call_target="tpu_custom_call" | custom-call | tf_op jit(solution)/shard_map/merge/pallas_call | solution.py:573
  169.6 1.7 %copy.18 = bf16[4,4,8192]{2,1,0:T(4,128)(2,1)} copy(bf16[4,4,8192]{2,1,0:T(4,128)(2,1)} %get-tuple-element.16) | data formatting | bytes 524288
  171.3 1.7 %copy.19 = bf16[4,4,8192]{2,1,0:T(4,128)(2,1)} copy(bf16[4,4,8192]{2,1,0:T(4,128)(2,1)} %get-tuple-element.17) | data formatting | bytes 524288
Async XLA Ops:
  0.6 99.8 %copy-start.1 = (s32[32,8]{0,1:T(8,128)S(1)}, s32[32,8]{0,1:T(8,128)}, u32[]{:S(2)}) copy-start(s32[32,8]{0,1:T(8,128)} %param.14) | copy-start | bytes 3076
  101.1 13.6 %copy-start = (bf16[8192]{0:T(1024)(128)(2,1)S(1)}, bf16[8192]{0:T(1024)(128)(2,1)}, u32[]{:S(2)}) copy-start(bf16[8192]{0:T(1024)(128)(2,1)} %param.21) | copy-start | bytes 49156

commit v3 on v2

--- a/solution.py
+++ b/solution.py
@@ -25,7 +25,9 @@
 QMAX = 128
 HELD = 16
 CHUNKS = 4
-PER = HELD // CHUNKS
+PART = CTOK // 4 // CHUNKS
+CAP = 8
+PLACES = 5 * HELD + 3 * CAP
 RING = 8
 WIDTH = D // RING
 ROWS = QMAX * GROUP
@@ -57,8 +59,8 @@
 
 
 def spread_kernel(
-    kv, queries, new_kv, cosines, sines, w, kv_all, q_all, fresh_all, w_all,
-    q_wide, q, fresh_wide, fresh, own_sem, kv_send, kv_recv, q_send, q_recv, f_send, f_recv, w_send, w_recv, z_send, z_recv,
+    retrieval, kv, queries, new_kv, cosines, sines, w, kv_all, q_all, fresh_all, w_all,
+    q_wide, q, fresh_wide, fresh, near, packed, packed_far, relay, near_sem, own_sem, kv_send, kv_recv, q_send, q_recv, f_send, f_recv, w_send, w_recv, z_send, z_recv,
 ):
     m = lax.axis_index("mp")
     z = lax.axis_index("store")
@@ -73,8 +75,8 @@
         return carry
 
     lax.fori_loop(1, SHARDS, greet, 0)
-    for near in (left, right):
-        pl.semaphore_signal(barrier, 1, device_id={"store": near}, device_id_type=MESH)
+    for beside in (left, right):
+        pl.semaphore_signal(barrier, 1, device_id={"store": beside}, device_id_type=MESH)
     pl.semaphore_wait(barrier, SHARDS + 1)
 
     def remote(src, dst, send, recv, **where):
@@ -82,58 +84,48 @@
             src_ref=src, dst_ref=dst, send_sem=send, recv_sem=recv, device_id=where, device_id_type=MESH
         )
 
-    def kv_rows(c, head):
-        return kv_all.at[z, pl.ds(PER * c, PER), pl.ds(pl.multiple_of(16 * head, 16), 16), :]
-
-    def kv_part(c, head):
-        return kv.at[pl.ds(PER * c, PER), :, pl.ds(pl.multiple_of(2 * HD * head, 2 * HD), 2 * HD)]
-
-    def kv_copy(c, i):
-        to = ahead(k, i, KVH)
-        return remote(
-            kv_part(c, to), kv_rows(c, k), kv_send.at[c, i], kv_recv.at[c, k], mp=QUARTERS * to + j
-        )
-
-    def kv_arrival(c, i):
-        come = ahead(k, i, KVH)
-        return remote(
-            kv_part(c, come), kv_rows(c, come), kv_send.at[c, i], kv_recv.at[c, come], mp=QUARTERS * come + j
-        )
-
-    def own_kv(c):
-        return pltpu.make_async_copy(kv_part(c, k), kv_rows(c, k), own_sem.at[c])
+    def kv_rows(i):
+        return kv_all.at[pl.ds(0, HELD), pl.ds(16 * i, 16), :]
+
+    def kv_part(head):
+        return kv.at[:, :, pl.ds(pl.multiple_of(2 * HD * head, 2 * HD), 2 * HD)]
+
+    def kv_copy(i):
+        to = ahead(k, KVH - i, KVH)
+        return remote(kv_part(to), kv_rows(i), kv_send.at[i], kv_recv.at[i], mp=QUARTERS * to + j)
+
+    own_kv = pltpu.make_async_copy(kv_part(k), kv_rows(0), own_sem.at[2])
+    own_kv.start()
+    for i in range(1, KVH):
+        kv_copy(i).start()
+
+    target = (right, left)
+
+    def rows_of(c):
+        return pl.ds(PART * c, PART)
+
+    def held(base, count, c):
+        return kv_all.at[pl.ds(base, count), rows_of(c)]
+
+    def z_copy(way, s, c):
+        if s == 0:
+            src, dst = held(0, HELD, c), held(HELD * (1 + way), HELD, c)
+        elif s == 1:
+            src, dst = held(HELD * (1 + way), HELD, c), near[way * CHUNKS + c]
+        elif s == 2:
+            src, dst = packed.at[way, c], held(5 * HELD + CAP * way, CAP, c)
+        elif s == 3:
+            src, dst = packed_far.at[way, c % 2], relay.at[way, c % 2]
+        else:
+            src, dst = relay.at[way, c % 2], held(5 * HELD + 2 * CAP, CAP, c)
+        return remote(src, dst, z_send.at[way, s, c], z_recv.at[way, s, c], store=target[way])
 
     for c in range(CHUNKS):
-        own_kv(c).start()
-
-        def send_kv(i, carry):
-            kv_copy(c, i).start()
-            return carry
-
-        lax.fori_loop(1, KVH, send_kv, 0)
-
-    def z_copy(way, s, c):
-        owner = ahead(z, (STORES - s) if way == 0 else s, STORES)
-        slab = kv_all.at[owner, pl.ds(PER * c, PER)]
-        return remote(
-            slab, slab, z_send.at[way, s, c], z_recv.at[way, s, c], store=right if way == 0 else left
-        )
-
-    def z_arrival(way, s, c):
-        owner = ahead(z, (STORES - 1 - s) if way == 0 else (s + 1), STORES)
-        slab = kv_all.at[owner, pl.ds(PER * c, PER)]
-        return remote(
-            slab, slab, z_send.at[way, s, c], z_recv.at[way, s, c], store=right if way == 0 else left
-        )
-
-    for c in range(CHUNKS):
-        own_kv(c).wait()
-
-        def take_kv(i, carry):
-            kv_arrival(c, i).wait_recv()
-            return carry
-
-        lax.fori_loop(1, KVH, take_kv, 0)
+        if c == 0:
+            own_kv.wait()
+        else:
+            kv_copy(2 * c).wait_recv()
+        kv_copy(2 * c + 1).wait_recv()
         for way in range(2):
             z_copy(way, 0, c).start()
 
@@ -171,8 +163,8 @@
         return remote(w_part(come), w_all.at[come], w_send.at[i], w_recv.at[come], mp=ring + come)
 
     own = [
-        pltpu.make_async_copy(fresh_part(k), fresh_all.at[k], own_sem.at[CHUNKS]),
-        pltpu.make_async_copy(q.at[k], q_all.at[:, m], own_sem.at[CHUNKS + 1]),
+        pltpu.make_async_copy(fresh_part(k), fresh_all.at[k], own_sem.at[0]),
+        pltpu.make_async_copy(q.at[k], q_all.at[:, m], own_sem.at[1]),
     ]
 
     def loop(low, high, act):
@@ -206,20 +198,55 @@
     loop(1, KVH, lambda i: f_copy(i).start())
     loop(1, SHARDS, lambda i: q_copy(i).start())
 
-    last = STORES // 2 - 1
+    def wanted(dest, source):
+        def look(n, carry):
+            count, picks = carry
+            found = retrieval[lax.rem(n, R), dest * REQ + n // R]
+            hit = (found >> 4) == source
+            picks = tuple(
+                jnp.where(hit & (count == at), found & (HELD - 1), pick) for at, pick in enumerate(picks)
+            )
+            return jnp.where(hit, count + 1, count), picks
+
+        zero = jnp.int32(0)
+        return lax.fori_loop(0, REQ * R, look, (zero, (zero,) * CAP))[1]
+
+    picks = [wanted(ahead(z, 1, STORES), ahead(z, 6, STORES)), wanted(ahead(z, 7, STORES), ahead(z, 2, STORES))]
+    far_picks = [wanted(ahead(z, 2, STORES), ahead(z, 6, STORES)), wanted(ahead(z, 6, STORES), ahead(z, 2, STORES))]
+
     halves = (range(CHUNKS // 2), range(CHUNKS // 2, CHUNKS))
-    for s in range(1, last + 1):
-        for c in range(CHUNKS):
-            for way in range(2):
-                if s < last or c in halves[way]:
-                    z_arrival(way, s - 1, c).wait_recv()
-                    z_copy(way, s, c).start()
-    for way in range(2):
-        for c in range(CHUNKS):
+    for c in range(CHUNKS):
+        for way in range(2):
+            z_copy(way, 0, c).wait_recv()
+            z_copy(way, 1, c).start()
+
+    def keep(way, c):
+        return pltpu.make_async_copy(
+            near[way * CHUNKS + c], held(HELD * (3 + way), HELD, c), near_sem.at[way, c]
+        )
+
+    for c in range(CHUNKS):
+        for way in range(2):
+            z_copy(way, 1, c).wait_recv()
+            source = near[way * CHUNKS + c]
+            for at in range(CAP):
+                packed[way, c, at] = source[picks[way][at]]
+            z_copy(way, 2, c).start()
             if c in halves[way]:
-                z_arrival(way, last, c).wait_recv()
-            else:
-                z_arrival(way, last - 1, c).wait_recv()
+                for at in range(CAP):
+                    packed_far[way, c % 2, at] = source[far_picks[way][at]]
+                z_copy(way, 3, c).start()
+            keep(way, c).start()
+    for n in range(CHUNKS // 2):
+        for way in range(2):
+            z_copy(way, 3, halves[way][n]).wait_recv()
+            z_copy(way, 4, halves[way][n]).start()
+    for c in range(CHUNKS):
+        for way in range(2):
+            keep(way, c).wait()
+            z_copy(way, 2, c).wait_recv()
+            if c in halves[way]:
+                z_copy(way, 4, c).wait_recv()
 
     for copy in own:
         copy.wait()
@@ -229,60 +256,79 @@
     loop(1, RING, lambda i: w_copy(i).wait_send())
     loop(1, KVH, lambda i: f_copy(i).wait_send())
     loop(1, SHARDS, lambda i: q_copy(i).wait_send())
-    for c in range(CHUNKS):
-        loop(1, KVH, lambda i: kv_copy(c, i).wait_send())
+    for i in range(1, KVH):
+        kv_copy(i).wait_send()
     for way in range(2):
-        for s in range(last + 1):
-            for c in range(CHUNKS):
-                if s < last or c in halves[way]:
+        for c in range(CHUNKS):
+            for s in (0, 1, 2):
+                z_copy(way, s, c).wait_send()
+            if c in halves[way]:
+                for s in (3, 4):
                     z_copy(way, s, c).wait_send()
 
 
-def spread(kv, queries, new_kv, cosines, sines, w):
+def spread(retrieval, kv, queries, new_kv, cosines, sines, w):
     bf, f32 = jnp.bfloat16, jnp.float32
     dma = pltpu.SemaphoreType.DMA
     return pl.pallas_call(
         spread_kernel,
         out_shape=(
-            jax.ShapeDtypeStruct((STORES, HELD, CTOK // QUARTERS, 2 * HD), bf),
+            jax.ShapeDtypeStruct((PLACES, CTOK // QUARTERS, 2 * HD), bf),
             jax.ShapeDtypeStruct((REQ, SHARDS, QMAX // SHARDS * GROUP, HD), bf),
             jax.ShapeDtypeStruct((KVH, 16, 2 * HD), bf),
             jax.ShapeDtypeStruct((RING, D // SHARDS, WIDTH), bf),
         ),
-        in_specs=[HBM] + [VMEM] * 4 + [HBM],
+        in_specs=[SMEM, HBM] + [VMEM] * 4 + [HBM],
         out_specs=(HBM,) * 4,
         scratch_shapes=[
             pltpu.VMEM((KVH, REQ, TOKENS * GROUP, HD), f32),
             pltpu.VMEM((KVH, REQ, TOKENS * GROUP, HD), bf),
             pltpu.VMEM((OWNED, KVH * 2 * HD), f32),
             pltpu.VMEM((OWNED, KVH * 2 * HD), bf),
-            dma((CHUNKS + 2,)),
-            dma((CHUNKS, KVH)), dma((CHUNKS, KVH)),
+            [pltpu.VMEM((HELD, PART, 2 * HD), bf)] * (2 * CHUNKS),
+            pltpu.VMEM((2, CHUNKS, CAP, PART, 2 * HD), bf),
+            pltpu.VMEM((2, CHUNKS // 2, CAP, PART, 2 * HD), bf),
+            pltpu.VMEM((2, CHUNKS // 2, CAP, PART, 2 * HD), bf),
+            dma((2, CHUNKS)),
+            dma((3,)),
+            dma((KVH,)), dma((KVH,)),
             dma((SHARDS,)), dma((SHARDS,)),
             dma((KVH,)), dma((KVH,)),
             dma((RING,)), dma((RING,)),
-            dma((2, STORES // 2, CHUNKS)), dma((2, STORES // 2, CHUNKS)),
+            dma((2, 5, CHUNKS)), dma((2, 5, CHUNKS)),
         ],
         compiler_params=pltpu.CompilerParams(
             collective_id=0, has_side_effects=True, vmem_limit_bytes=60 << 20
         ),
         name="spread",
-    )(kv, queries, new_kv, cosines, sines, w)
+    )(retrieval, kv, queries, new_kv, cosines, sines, w)
 
 
 def attend_kernel(
     retrieval, places, lengths, cosines, sines, q_all, fresh_all, kv_all, out, lse,
-    slots, keys, q, fresh, sem, q_sem, fresh_sem,
+    slots, keys, q, fresh, counts, sem, q_sem, fresh_sem,
 ):
     quarter = CTOK // QUARTERS
     held = R * quarter
     j = lax.rem(lax.axis_index("mp"), QUARTERS)
     z = lax.axis_index("store")
 
-    def fetch(b, r):
+    def fetch(b, r, place=0):
         return pltpu.make_async_copy(
-            kv_all.at[retrieval[z * REQ + b, r]], slots.at[b, pl.ds(r * quarter, quarter)], sem.at[b, r]
-        )
+            kv_all.at[place], slots.at[b, pl.ds(r * quarter, quarter)], sem.at[b, r]
+        )
+
+    for s in range(STORES):
+        counts[s] = 0
+
+    def locate(b, r):
+        found = retrieval[r, z * REQ + b]
+        apart = ((found >> 4) - z) & (STORES - 1)
+        rank = counts[apart]
+        counts[apart] = rank + 1
+        near = HELD * jnp.where(apart <= 2, 2 * apart, 2 * (STORES - apart) - 1) + (found & (HELD - 1))
+        far = 5 * HELD + CAP * jnp.where(apart == 5, 0, jnp.where(apart == 3, 1, 2)) + rank
+        return jnp.where((apart <= 2) | (apart >= 6), near, far)
 
     def fetch_q(b):
         return pltpu.make_async_copy(q_all.at[b], q.at[b], q_sem.at[b])
@@ -290,7 +336,7 @@
     fetch_fresh = pltpu.make_async_copy(fresh_all, fresh, fresh_sem)
     for b in range(REQ):
         for r in range(R):
-            fetch(b, r).start()
+            fetch(b, r, locate(b, r)).start()
         fetch_q(b).start()
         if b == 0:
             fetch_fresh.start()
@@ -364,6 +410,7 @@
             pltpu.VMEM(((R + 1) * quarter, HD), bf),
             pltpu.VMEM((REQ, ROWS, HD), bf),
             pltpu.VMEM((quarter, 2 * HD), bf),
+            pltpu.SMEM((STORES,), jnp.int32),
             dma((REQ, R)), dma((REQ,)), dma,
         ],
         compiler_params=pltpu.CompilerParams(vmem_limit_bytes=60 << 20),
@@ -607,14 +654,15 @@
     context = R * CTOK
     cos_own, sin_own = turns(np.arange(context, context + QMAX))
     shape = (SHARDS, TOKENS, HD)
+    wanted = jnp.transpose(retrieval)
     kv_all, q_all, fresh_all, w_all = spread(
-        kv_store, queries, new_kv, cos_own.reshape(shape), sin_own.reshape(shape), out_weight
+        wanted, kv_store, queries, new_kv, cos_own.reshape(shape), sin_own.reshape(shape), out_weight
     )
     cos_at, sin_at = turns(np.arange(R) * CTOK)
     part, lse = attend(
-        retrieval, positions, lengths, cos_at, sin_at, q_all.reshape(REQ, ROWS, HD),
+        wanted, positions, lengths, cos_at, sin_at, q_all.reshape(REQ, ROWS, HD),
         fresh_all.reshape(KVH * 16, 2 * HD),
-        kv_all.reshape(STORES * HELD, CTOK // QUARTERS, 2 * HD),
+        kv_all,
     )
     return merge(part, lse, out_weight, w_all, hidden, norm_gain.reshape(1, D))
 

time: 173 us -> 164 us (0.948)
  Pallas kernels: 168 us -> 158 us
    pallas_call x1, Pallas kernels: 99.7 us -> 89.3 us  [spread(): pl.pallas_call(spread_kernel, out_shape=(jax.ShapeDtypeStruct((PLACES, CT...]
    unnamed x7 -> x4, local copies, waits for them, and re-layouts: 4.18 us -> 3.49 us
where the time goes in v3:
time: 164 us; the launch traced here: 163 us
  Pallas kernels  158 us (96%)
  local copies, waits for them, and re-layouts  4.13 us (3%)
    pallas_call x1, Pallas kernels, spread(): pl.pallas_call(spread_kernel, out_shape=(jax.ShapeDtypeStruct((PLACES, CT...  89.3 us
    pallas_call x1, Pallas kernels, merge(): pl.pallas_call(merge_kernel, out_shape=(jax.ShapeDtypeStruct((REQ, TOKENS...  55.3 us
    pallas_call x1, Pallas kernels, attend(): pl.pallas_call(attend_kernel, out_shape=(jax.ShapeDtypeStruct((REQ, ROWS,...  13.3 us
    unnamed x4, local copies, waits for them, and re-layouts  3.49 us

profile of v3, /device:TPU:1, one launch (start us, length us, event | category | flops | bytes accessed | tf_op | source)
XLA Modules:
  0.0 162.7 jit_solution(1972514533349073867)
XLA Ops:
  0.6 89.3 %spread.1 = (bf16[104,128,256]{2,1,0:T(8,128)(2,1)}, bf16[4,32,32,128]{3,2,1,0:T(8,128)(2,1)}, bf16[8,16,256]{2,1,0:T(8,128)(2,1)}, bf16[8,256,1024]{2,1,0:T(8,128)(2,1)}) custom-call(s32[8,32]{1,0:T(8,128)} %bitcast.5, bf16[16,16,2048]{2,1,0:T(8,128)(2,1)} %kv.1, bf16[4,4,8192]{2,1,0:T(4,128)(2,1)} %queries.1, bf16[4,4,2048]{2,1,0:T(4,128)(2,1)} %new_kv.1, ...), custom_call_target="tpu_custom_call" | custom-call | tf_op jit(solution)/shard_map/spread/pallas_call | solution.py:273
  90.0 0.0 copy-start
  90.0 13.3 %attend.1 = (bf16[4,1024,128]{2,1,0:T(8,128)(2,1)}, f32[4,8,1024]{2,1,0:T(8,128)}) custom-call(s32[8,32]{1,0:T(8,128)} %bitcast.6, s32[4,8]{1,0:T(4,128)} %places.1, s32[4]{0:T(128)} %lengths.1, f32[8,128]{1,0:T(8,128)} %constant.10.clone.cosines, f32[8,128]{1,0:T(8,128)} %constant.11.clone.sines, bf16[4,1024,128]{2,1,0:T(8,128)(2,1)} %bitcast.3, ...), custom_call_target="tpu_custom_call" | custom-call | tf_op jit(solution)/shard_map/attend/pallas_call | solution.py:400
  103.3 0.0 copy-done
  103.3 0.6 reshape.23.gain
  103.9 55.3 %merge.1 = (bf16[4,4,8192]{2,1,0:T(4,128)(2,1)}, bf16[4,4,8192]{2,1,0:T(4,128)(2,1)}) custom-call(bf16[4,1024,128]{2,1,0:T(8,128)(2,1)} %get-tuple-element.11.part, f32[4,8,1024]{2,1,0:T(8,128)} %get-tuple-element.12.lse, bf16[256,8192]{1,0:T(8,128)(2,1)} %w_own.1, bf16[8,256,1024]{2,1,0:T(8,128)(2,1)} %get-tuple-element.13.w_all, ...), custom_call_target="tpu_custom_call" | custom-call | tf_op jit(solution)/shard_map/merge/pallas_call | solution.py:620
  159.2 1.7 %copy.17 = bf16[4,4,8192]{2,1,0:T(4,128)(2,1)} copy(bf16[4,4,8192]{2,1,0:T(4,128)(2,1)} %get-tuple-element.16) | data formatting | bytes 524288
  161.0 1.7 %copy.18 = bf16[4,4,8192]{2,1,0:T(4,128)(2,1)} copy(bf16[4,4,8192]{2,1,0:T(4,128)(2,1)} %get-tuple-element.17) | data formatting | bytes 524288
Async XLA Ops:
  90.0 13.3 %copy-start = (bf16[8192]{0:T(1024)(128)(2,1)S(1)}, bf16[8192]{0:T(1024)(128)(2,1)}, u32[]{:S(2)}) copy-start(bf16[8192]{0:T(1024)(128)(2,1)} %param.21) | copy-start | bytes 49156

commit v4 on v3

--- a/solution.py
+++ b/solution.py
@@ -27,11 +27,14 @@
 CHUNKS = 4
 PART = CTOK // 4 // CHUNKS
 CAP = 8
+WINDOW = 4
+EARLY = 3
 PLACES = 5 * HELD + 3 * CAP
 RING = 8
 WIDTH = D // RING
 ROWS = QMAX * GROUP
 BLOCK = 512
+SUB = 256
 TOKENS = QMAX // SHARDS
 OWNED = REQ * TOKENS
 LOG2E = 1.4426950408889634
@@ -60,7 +63,7 @@
 
 def spread_kernel(
     retrieval, kv, queries, new_kv, cosines, sines, w, kv_all, q_all, fresh_all, w_all,
-    q_wide, q, fresh_wide, fresh, near, packed, packed_far, relay, near_sem, own_sem, kv_send, kv_recv, q_send, q_recv, f_send, f_recv, w_send, w_recv, z_send, z_recv,
+    q_wide, q, fresh_wide, fresh, near, packed, packed_far, relay, near_sem, own_sem, kv_send, kv_recv, q_send, q_recv, f_send, f_recv, w_send, w_recv, o_send, o_recv, z_send, z_recv,
 ):
     m = lax.axis_index("mp")
     z = lax.axis_index("store")
@@ -95,9 +98,9 @@
         return remote(kv_part(to), kv_rows(i), kv_send.at[i], kv_recv.at[i], mp=QUARTERS * to + j)
 
     own_kv = pltpu.make_async_copy(kv_part(k), kv_rows(0), own_sem.at[2])
-    own_kv.start()
     for i in range(1, KVH):
         kv_copy(i).start()
+    own_kv.start()
 
     target = (right, left)
 
@@ -107,10 +110,13 @@
     def held(base, count, c):
         return kv_all.at[pl.ds(base, count), rows_of(c)]
 
+    def z_own(way, i):
+        src = kv_part(k) if i == 0 else kv_rows(i)
+        dst = kv_all.at[pl.ds(HELD * (1 + way), HELD), pl.ds(16 * i, 16), :]
+        return remote(src, dst, o_send.at[way, i], o_recv.at[way, i], store=target[way])
+
     def z_copy(way, s, c):
-        if s == 0:
-            src, dst = held(0, HELD, c), held(HELD * (1 + way), HELD, c)
-        elif s == 1:
+        if s == 1:
             src, dst = held(HELD * (1 + way), HELD, c), near[way * CHUNKS + c]
         elif s == 2:
             src, dst = packed.at[way, c], held(5 * HELD + CAP * way, CAP, c)
@@ -120,15 +126,6 @@
             src, dst = relay.at[way, c % 2], held(5 * HELD + 2 * CAP, CAP, c)
         return remote(src, dst, z_send.at[way, s, c], z_recv.at[way, s, c], store=target[way])
 
-    for c in range(CHUNKS):
-        if c == 0:
-            own_kv.wait()
-        else:
-            kv_copy(2 * c).wait_recv()
-        kv_copy(2 * c + 1).wait_recv()
-        for way in range(2):
-            z_copy(way, 0, c).start()
-
     def fresh_part(head):
         return fresh.at[:, pl.ds(pl.multiple_of(2 * HD * head, 2 * HD), 2 * HD)]
 
@@ -174,6 +171,22 @@
 
         lax.fori_loop(low, high, body, 0)
 
+    sent = ([], [])
+
+    def push(way, copy):
+        if len(sent[way]) >= WINDOW:
+            sent[way][-WINDOW].wait_send()
+        copy.start()
+        sent[way].append(copy)
+
+    def push_own(i):
+        if i > 0:
+            kv_copy(i).wait_recv()
+        for way in range(2):
+            push(way, z_own(way, i))
+
+    for i in range(EARLY):
+        push_own(i)
     loop(1, RING, lambda i: w_copy(i).start())
 
     cos, sin = cosines[m], sines[m]
@@ -183,7 +196,7 @@
             for g in range(GROUP):
                 at = pl.ds(pl.multiple_of((head * GROUP + g) * HD, HD), HD)
                 value = rotate(queries[b, :, at].astype(jnp.float32), cos, sin)
-                q_wide[head, b, pl.ds(g, TOKENS, stride=GROUP), :] = value
+                q_wide[head, b, pl.ds(g, TOKENS, stride=GROUP), :] = value * (HD**-0.5 * LOG2E)
             at = pl.multiple_of(2 * HD * head, 2 * HD)
             key = rotate(new_kv[b, :, pl.ds(at, HD)].astype(jnp.float32), cos, sin)
             fresh_wide[b * TOKENS : (b + 1) * TOKENS, pl.ds(at, HD)] = key
@@ -197,6 +210,9 @@
         copy.start()
     loop(1, KVH, lambda i: f_copy(i).start())
     loop(1, SHARDS, lambda i: q_copy(i).start())
+    for i in range(EARLY, KVH):
+        push_own(i)
+    own_kv.wait()
 
     def wanted(dest, source):
         def look(n, carry):
@@ -217,8 +233,9 @@
     halves = (range(CHUNKS // 2), range(CHUNKS // 2, CHUNKS))
     for c in range(CHUNKS):
         for way in range(2):
-            z_copy(way, 0, c).wait_recv()
-            z_copy(way, 1, c).start()
+            for i in range(2 * c, 2 * c + 2):
+                z_own(way, i).wait_recv()
+            push(way, z_copy(way, 1, c))
 
     def keep(way, c):
         return pltpu.make_async_copy(
@@ -231,16 +248,16 @@
             source = near[way * CHUNKS + c]
             for at in range(CAP):
                 packed[way, c, at] = source[picks[way][at]]
-            z_copy(way, 2, c).start()
+            push(way, z_copy(way, 2, c))
             if c in halves[way]:
                 for at in range(CAP):
                     packed_far[way, c % 2, at] = source[far_picks[way][at]]
-                z_copy(way, 3, c).start()
+                push(way, z_copy(way, 3, c))
             keep(way, c).start()
     for n in range(CHUNKS // 2):
         for way in range(2):
             z_copy(way, 3, halves[way][n]).wait_recv()
-            z_copy(way, 4, halves[way][n]).start()
+            push(way, z_copy(way, 4, halves[way][n]))
     for c in range(CHUNKS):
         for way in range(2):
             keep(way, c).wait()
@@ -258,13 +275,9 @@
     loop(1, SHARDS, lambda i: q_copy(i).wait_send())
     for i in range(1, KVH):
         kv_copy(i).wait_send()
-    for way in range(2):
-        for c in range(CHUNKS):
-            for s in (0, 1, 2):
-                z_copy(way, s, c).wait_send()
-            if c in halves[way]:
-                for s in (3, 4):
-                    z_copy(way, s, c).wait_send()
+    for copies in sent:
+        for copy in copies[-WINDOW:]:
+            copy.wait_send()
 
 
 def spread(retrieval, kv, queries, new_kv, cosines, sines, w):
@@ -295,6 +308,7 @@
             dma((SHARDS,)), dma((SHARDS,)),
             dma((KVH,)), dma((KVH,)),
             dma((RING,)), dma((RING,)),
+            dma((2, KVH)), dma((2, KVH)),
             dma((2, 5, CHUNKS)), dma((2, 5, CHUNKS)),
         ],
         compiler_params=pltpu.CompilerParams(
@@ -344,10 +358,10 @@
     for b in range(REQ):
         slots[b, held:, :] = fresh[...]
     keys[held:, :] = fresh[:, :HD]
-    col = lax.broadcasted_iota(jnp.int32, (BLOCK, quarter), 1)
+    col = lax.broadcasted_iota(jnp.int32, (SUB, quarter), 1)
     fresh_token = TOKENS * (QUARTERS * (col >> 4) + j) + (col & 3)
     fresh_request = (col >> 2) & 3
-    row = lax.broadcasted_iota(jnp.int32, (BLOCK, quarter), 0)
+    row = lax.broadcasted_iota(jnp.int32, (SUB, quarter), 0)
     for b in range(REQ):
         for r in range(R):
             fetch(b, r).wait()
@@ -360,26 +374,28 @@
         length = lengths[b]
 
         def block(i, carry):
-            span = pl.ds(pl.multiple_of(i * BLOCK, BLOCK), BLOCK)
-            scores = lax.dot_general(
-                q[b, span, :], keys[...], (((1,), (1,)), ((), ())), preferred_element_type=jnp.float32
-            ) * (HD**-0.5 * LOG2E)
-            allowed = (fresh_request == b) & (fresh_token <= ((i * BLOCK + row) >> 3))
-            fresh_scores = jnp.where(allowed, scores[:, held:], -1e30)
-            scores = scores[:, :held]
-            top = jnp.maximum(
-                jnp.max(scores, axis=1, keepdims=True), jnp.max(fresh_scores, axis=1, keepdims=True)
-            )
-            expo, fresh_expo = jnp.exp2(scores - top), jnp.exp2(fresh_scores - top)
-            total = jnp.sum(expo, axis=1, keepdims=True) + jnp.sum(fresh_expo, axis=1, keepdims=True)
-            sums = jnp.dot(
-                expo.astype(jnp.bfloat16), slots[b, :held, HD:], preferred_element_type=jnp.float32
-            ) + jnp.dot(
-                fresh_expo.astype(jnp.bfloat16), slots[b, held:, HD:], preferred_element_type=jnp.float32
-            )
-            out[b, span, :] = jnp.where(i * BLOCK + row < length * GROUP, sums / total, 0.0).astype(jnp.bfloat16)
-            logs = top + jnp.log(total) * LOG2E
-            lse[b, :, span] = jnp.broadcast_to(logs, (BLOCK, HD)).T[:8]
+            spans = [pl.ds(pl.multiple_of(i * BLOCK + n * SUB, SUB), SUB) for n in range(BLOCK // SUB)]
+            every = [
+                lax.dot_general(
+                    q[b, span, :], keys[...], (((1,), (1,)), ((), ())), preferred_element_type=jnp.float32
+                )
+                for span in spans
+            ]
+            for n, (span, scores) in enumerate(zip(spans, every)):
+                at = i * BLOCK + n * SUB + row
+                allowed = (fresh_request == b) & (fresh_token <= (at >> 3))
+                scores = jnp.concatenate(
+                    [scores[:, :held], jnp.where(allowed, scores[:, held:], -1e30)], axis=1
+                )
+                top = jnp.max(scores, axis=1, keepdims=True)
+                expo = jnp.exp2(scores - top)
+                total = jnp.sum(expo, axis=1, keepdims=True)
+                sums = jnp.dot(
+                    expo.astype(jnp.bfloat16), slots[b, :, HD:], preferred_element_type=jnp.float32
+                )
+                out[b, span, :] = jnp.where(at < length * GROUP, sums / total, 0.0).astype(jnp.bfloat16)
+                logs = top + jnp.log(total) * LOG2E
+                lse[b, :, span] = jnp.broadcast_to(logs, (SUB, HD)).T[:8]
             return carry
 
         def blank(i, carry):
@@ -419,8 +435,8 @@
 
 
 def merge_kernel(
-    part, lse, w_own, w_all, hidden, gain, residual, normed,
-    w, from_mate, from_mate_lse, pair, pair_lse, from_chip, from_chip_lse, rows, attended, sent, got, mixed,
+    part, lse, w_own, w_all, hidden, mixed,
+    w, from_mate, from_mate_lse, pair, pair_lse, from_chip, from_chip_lse, rows, attended, sent, got,
     w_sem, own_sem, c_send, c_recv, l_send, l_recv, g_send, g_recv, p_send, p_recv,
 ):
     m = lax.axis_index("mp")
@@ -587,19 +603,13 @@
     p_own().wait()
     loop(1, SHARDS, lambda i: p_arrival(ahead(m, i, SHARDS)).wait_recv())
 
-    square = jnp.zeros((owned, 1), jnp.float32)
     for c in range(RING):
         cols = slice(c * WIDTH, (c + 1) * WIDTH)
-        value = jnp.concatenate([hidden[b, :, cols].astype(jnp.float32) for b in range(REQ)], axis=0)
-        for group in range(SHARDS // RING):
+        value = got[c].astype(jnp.float32)
+        for group in range(1, SHARDS // RING):
             value = value + got[RING * group + c].astype(jnp.float32)
-        mixed[:, cols] = value
-        square = square + jnp.sum(value * value, axis=-1, keepdims=True)
-    factor = lax.rsqrt(square / D + eps_norm)
-    for b in range(REQ):
-        mine = slice(b * TOKENS, (b + 1) * TOKENS)
-        residual[b] = mixed[mine, :].astype(jnp.bfloat16)
-        normed[b] = (mixed[mine, :] * factor[mine] * gain[...].astype(jnp.float32)).astype(jnp.bfloat16)
+        for b in range(REQ):
+            mixed[b, :, cols] = value[b * TOKENS : (b + 1) * TOKENS] + hidden[b, :, cols].astype(jnp.float32)
 
     for at, n in order:
         for copy in mate_copies(at, n):
@@ -613,15 +623,15 @@
     loop(1, SHARDS, lambda i: p_copy(ahead(m, i, SHARDS)).wait_send())
 
 
-def merge(part, lse, w_own, w_all, hidden, gain):
+def merge(part, lse, w_own, w_all, hidden):
     bf, f32 = jnp.bfloat16, jnp.float32
     dma = pltpu.SemaphoreType.DMA
     owned = OWNED
     return pl.pallas_call(
         merge_kernel,
-        out_shape=(jax.ShapeDtypeStruct((REQ, TOKENS, D), bf),) * 2,
-        in_specs=[VMEM, VMEM, HBM, HBM, VMEM, VMEM],
-        out_specs=(VMEM, VMEM),
+        out_shape=jax.ShapeDtypeStruct((REQ, TOKENS, D), f32),
+        in_specs=[VMEM, VMEM, HBM, HBM, VMEM],
+        out_specs=VMEM,
         scratch_shapes=[
             pltpu.VMEM((RING, D // SHARDS, WIDTH), bf),
             pltpu.VMEM((2, ROWS, HD), bf),
@@ -634,7 +644,6 @@
             pltpu.VMEM((RING, QMAX, GROUP * HD), bf),
             pltpu.VMEM((REQ * QMAX, WIDTH), bf),
             pltpu.VMEM((SHARDS, owned, WIDTH), bf),
-            pltpu.VMEM((owned, D), f32),
             dma((RING,)), dma,
             dma((3,)), dma((3,)),
             dma((3,)), dma((3,)),
@@ -642,10 +651,10 @@
             dma((SHARDS,)), dma((SHARDS,)),
         ],
         compiler_params=pltpu.CompilerParams(
-            collective_id=1, has_side_effects=True, vmem_limit_bytes=60 << 20
+            collective_id=1, has_side_effects=True, vmem_limit_bytes=52 << 20
         ),
         name="merge",
-    )(part, lse, w_own, w_all, hidden, gain)
+    )(part, lse, w_own, w_all, hidden)
 
 
 def on_device(
@@ -664,7 +673,10 @@
         fresh_all.reshape(KVH * 16, 2 * HD),
         kv_all,
     )
-    return merge(part, lse, out_weight, w_all, hidden, norm_gain.reshape(1, D))
+    mixed = merge(part, lse, out_weight, w_all, hidden)
+    square = jnp.mean(mixed * mixed, axis=-1, keepdims=True)
+    normed = mixed * lax.rsqrt(square + eps_norm) * norm_gain.astype(jnp.float32)
+    return mixed.astype(jnp.bfloat16), normed.astype(jnp.bfloat16)
 
 
 def solution(mesh):

time: 164 us -> 155 us (0.945)
  Pallas kernels: 158 us -> 151 us
  local copies, waits for them, and re-layouts: 4.13 us -> 2.13 us
    pallas_call x1, Pallas kernels: 55.3 us -> 52.8 us  [merge(): pl.pallas_call(merge_kernel, out_shape=jax.ShapeDtypeStruct((REQ, TOKENS,...]
    pallas_call x1, Pallas kernels: 13.3 us -> 11 us  [attend(): pl.pallas_call(attend_kernel, out_shape=(jax.ShapeDtypeStruct((REQ, ROWS,...]
    pallas_call x1, Pallas kernels: 89.3 us -> 87.3 us  [spread(): pl.pallas_call(spread_kernel, out_shape=(jax.ShapeDtypeStruct((PLACES, CT...]
    unnamed x4 -> x8, local copies, waits for them, and re-layouts: 3.49 us -> 2.13 us
where the time goes in v4:
time: 155 us
  Pallas kernels  151 us (97%)
  local copies, waits for them, and re-layouts  2.13 us (1%)
    pallas_call x1, Pallas kernels, spread(): pl.pallas_call(spread_kernel, out_shape=(jax.ShapeDtypeStruct((PLACES, CT...  87.3 us
    pallas_call x1, Pallas kernels, merge(): pl.pallas_call(merge_kernel, out_shape=jax.ShapeDtypeStruct((REQ, TOKENS,...  52.8 us
    pallas_call x1, Pallas kernels, attend(): pl.pallas_call(attend_kernel, out_shape=(jax.ShapeDtypeStruct((REQ, ROWS,...  11 us

profile of v4, /device:TPU:1, one launch (start us, length us, event | category | flops | bytes accessed | tf_op | source)
XLA Modules:
  0.0 155.1 jit_solution(4223497972691871727)
XLA Ops:
  0.6 87.3 %spread.1 = (bf16[104,128,256]{2,1,0:T(8,128)(2,1)}, bf16[4,32,32,128]{3,2,1,0:T(8,128)(2,1)}, bf16[8,16,256]{2,1,0:T(8,128)(2,1)}, bf16[8,256,1024]{2,1,0:T(8,128)(2,1)}) custom-call(s32[8,32]{1,0:T(8,128)} %bitcast.5, bf16[16,16,2048]{2,1,0:T(8,128)(2,1)} %kv.1, bf16[4,4,8192]{2,1,0:T(4,128)(2,1)} %queries.1, bf16[4,4,2048]{2,1,0:T(4,128)(2,1)} %new_kv.1, ...), custom_call_target="tpu_custom_call" | custom-call | tf_op jit(solution)/shard_map/spread/pallas_call | solution.py:286
  87.9 0.0 copy-start.1
  87.9 11.0 %attend.1 = (bf16[4,1024,128]{2,1,0:T(8,128)(2,1)}, f32[4,8,1024]{2,1,0:T(8,128)}) custom-call(s32[8,32]{1,0:T(8,128)} %bitcast.6, s32[4,8]{1,0:T(4,128)} %places.1, s32[4]{0:T(128)} %lengths.1, f32[8,128]{1,0:T(8,128)} %constant.17.clone.cosines, f32[8,128]{1,0:T(8,128)} %constant.18.clone.sines, bf16[4,1024,128]{2,1,0:T(8,128)(2,1)} %bitcast.3, ...), custom_call_target="tpu_custom_call" | custom-call | tf_op jit(solution)/shard_map/attend/pallas_call | solution.py:416
  98.9 0.0 copy-done.1
  99.0 0.0 copy-start
  99.0 1.2 copy-done
  100.2 0.0 copy-start.2
  100.2 0.9 copy-done.2
  101.1 0.0 copy-start.3
  101.1 52.8 %merge.1 = f32[4,4,8192]{2,1,0:T(4,128)S(1)} custom-call(bf16[4,1024,128]{2,1,0:T(8,128)(2,1)S(1)} %copy-done, f32[4,8,1024]{2,1,0:T(8,128)S(1)} %copy-done.2, bf16[256,8192]{1,0:T(8,128)(2,1)} %w_own.1, bf16[8,256,1024]{2,1,0:T(8,128)(2,1)} %get-tuple-element.13.w_all, bf16[4,4,8192]{2,1,0:T(4,128)(2,1)S(1)} %copy-done.1), custom_call_target="tpu_custom_call" | custom-call | tf_op jit(solution)/shard_map/merge/pallas_call | solution.py:630
  153.9 0.2 multiply_reduce_fusion
  154.1 0.0 copy-done.3
  154.1 1.0 multiply_convert_fusion
  (2 shorter events, 0.0 us)
Async XLA Ops:
  87.9 11.0 %copy-start.1 = (bf16[4,4,8192]{2,1,0:T(4,128)(2,1)S(1)}, bf16[4,4,8192]{2,1,0:T(4,128)(2,1)}, u32[]{:S(2)}) copy-start(bf16[4,4,8192]{2,1,0:T(4,128)(2,1)} %hidden.1) | copy-start | bytes 786436
  99.0 1.2 copy-start
  100.2 0.9 copy-start.2
  101.1 53.0 %copy-start.3 = (bf16[8192]{0:T(1024)(128)(2,1)S(1)}, bf16[8192]{0:T(1024)(128)(2,1)}, u32[]{:S(2)}) copy-start(bf16[8192]{0:T(1024)(128)(2,1)} %param.21) | copy-start | bytes 49156

commit v5 on v4

--- a/solution.py
+++ b/solution.py
@@ -33,6 +33,7 @@
 RING = 8
 WIDTH = D // RING
 ROWS = QMAX * GROUP
+HALF = ROWS // 2
 BLOCK = 512
 SUB = 256
 TOKENS = QMAX // SHARDS
@@ -482,70 +483,86 @@
 
     def mate_copies(at, n):
         give = 1 - core + 2 * at
+        span = pl.ds(n // 2 * HALF, HALF)
         return (
-            remote(lse.at[give], from_mate_lse.at[at], l_send.at[n], l_recv.at[n], mate),
-            remote(part.at[give], from_mate.at[at], c_send.at[n], c_recv.at[n], mate),
+            remote(lse.at[give, :, span], from_mate_lse.at[at, :, span], l_send.at[n], l_recv.at[n], mate),
+            remote(part.at[give, span], from_mate.at[at, span], c_send.at[n], c_recv.at[n], mate),
+        )
+
+    def chip_copies(n):
+        span = pl.ds(n * HALF, HALF)
+        return (
+            remote(pair_lse.at[:, span], from_chip_lse.at[:, span], l_send.at[4 + n], l_recv.at[4 + n], chip),
+            remote(pair.at[span], from_chip.at[span], c_send.at[4 + n], c_recv.at[4 + n], chip),
         )
 
     def combine(one, one_log, two, two_log):
         top = jnp.maximum(one_log, two_log)
         one_share, two_share = jnp.exp2(one_log - top), jnp.exp2(two_log - top)
         total = one_share + two_share
-        share = jnp.broadcast_to(one_share / total, (HD, ROWS)).T
+        share = jnp.broadcast_to(one_share / total, (HD, HALF)).T
         return two + (one - two) * share, top + jnp.log(total) * LOG2E
 
-    def wide(ref, at):
-        return ref[at].astype(jnp.float32)
-
-    pair_copies = (
-        remote(pair_lse, from_chip_lse, l_send.at[2], l_recv.at[2], chip),
-        remote(pair, from_chip, c_send.at[2], c_recv.at[2], chip),
-    )
+    def with_mate(at, n):
+        span = slice(n * HALF, (n + 1) * HALF)
+        keep = core + 2 * at
+        return combine(
+            part[keep, span].astype(jnp.float32), lse[keep, :1, span],
+            from_mate[at, span].astype(jnp.float32), from_mate_lse[at, :1, span],
+        )
+
+    def g_copy(at, n, hf, to):
+        block = attended.at[at, pl.ds(hf * (QMAX // 2), QMAX // 2)]
+        return remote(block, block, g_send.at[hf, n], g_recv.at[hf, n], to)
+
     other = 1 - half
     order = ((other, 0), (half, 1))
-    for at, n in order:
-        for copy in mate_copies(at, n):
-            copy.start()
-    for copy in mate_copies(other, 0):
-        copy.wait_recv()
-    give = core + 2 * other
-    value, logs = combine(
-        wide(part, give), lse[give, :1, :], wide(from_mate, other), from_mate_lse[other, :1, :]
-    )
-    pair[...] = value.astype(jnp.bfloat16)
-    pair_lse[...] = jnp.broadcast_to(logs, (8, ROWS))
-    for copy in pair_copies:
-        copy.start()
-    for copy in mate_copies(half, 1):
-        copy.wait_recv()
-    value, logs = combine(
-        wide(part, j), lse[j, :1, :], wide(from_mate, half), from_mate_lse[half, :1, :]
-    )
-    rows[...] = value
-    for copy in pair_copies:
-        copy.wait_recv()
-    value, logs = combine(rows[...], logs, from_chip[...].astype(jnp.float32), from_chip_lse[:1, :])
-    rows[...] = value
-    for h in range(GROUP):
-        attended[place, :, h * HD : (h + 1) * HD] = rows[pl.ds(h, QMAX, stride=GROUP), :].astype(jnp.bfloat16)
-
-    def g_copy(at, n, to):
-        return remote(attended.at[at], attended.at[at], g_send.at[n], g_recv.at[n], to)
-
     hops = (2, 6, 4)
     mate_place = place + 1 - 2 * core
-    g_copy(place, 0, mate).start()
-    for n, hop in enumerate(hops):
-        g_copy(place, 1 + n, ring + ahead(place, hop, RING)).start()
+    for hf in range(2):
+        for at, n in order:
+            for copy in mate_copies(at, 2 * hf + n):
+                copy.start()
+    for hf in range(2):
+        for copy in mate_copies(other, 2 * hf):
+            copy.wait_recv()
+        value, logs = with_mate(other, hf)
+        pair[hf * HALF : (hf + 1) * HALF, :] = value.astype(jnp.bfloat16)
+        pair_lse[:, hf * HALF : (hf + 1) * HALF] = jnp.broadcast_to(logs, (8, HALF))
+        for copy in chip_copies(hf):
+            copy.start()
+    kept = []
+    for hf in range(2):
+        for copy in mate_copies(half, 2 * hf + 1):
+            copy.wait_recv()
+        value, logs = with_mate(half, hf)
+        rows[hf * HALF : (hf + 1) * HALF, :] = value
+        kept.append(logs)
+    for hf in range(2):
+        span = slice(hf * HALF, (hf + 1) * HALF)
+        for copy in chip_copies(hf):
+            copy.wait_recv()
+        rows[span, :] = combine(
+            rows[span, :], kept[hf], from_chip[span].astype(jnp.float32), from_chip_lse[:1, span]
+        )[0]
+        for h in range(GROUP):
+            attended[place, hf * (QMAX // 2) : (hf + 1) * (QMAX // 2), h * HD : (h + 1) * HD] = rows[
+                pl.ds(hf * HALF + h, QMAX // 2, stride=GROUP), :
+            ].astype(jnp.bfloat16)
+        for n, hop in enumerate(hops):
+            g_copy(place, 1 + n, hf, ring + ahead(place, hop, RING)).start()
+        g_copy(place, 0, hf, mate).start()
     for load in w_loads:
         load.wait()
-    for n, hop in enumerate(hops):
-        come = ahead(place, RING - hop, RING)
-        g_copy(come, 1 + n, mate).wait_recv()
-        g_copy(come, 4 + n, mate).start()
-    g_copy(mate_place, 0, mate).wait_recv()
-    for n, hop in enumerate(hops):
-        g_copy(ahead(mate_place, RING - hop, RING), 4 + n, mate).wait_recv()
+    for hf in range(2):
+        for n, hop in enumerate(hops):
+            come = ahead(place, RING - hop, RING)
+            g_copy(come, 1 + n, hf, mate).wait_recv()
+            g_copy(come, 4 + n, hf, mate).start()
+    for hf in range(2):
+        g_copy(mate_place, 0, hf, mate).wait_recv()
+        for n, hop in enumerate(hops):
+            g_copy(ahead(mate_place, RING - hop, RING), 4 + n, hf, mate).wait_recv()
 
     owned = OWNED
     span = REQ * QMAX // 4
@@ -611,15 +628,16 @@
         for b in range(REQ):
             mixed[b, :, cols] = value[b * TOKENS : (b + 1) * TOKENS] + hidden[b, :, cols].astype(jnp.float32)
 
-    for at, n in order:
-        for copy in mate_copies(at, n):
+    for hf in range(2):
+        for at, n in order:
+            for copy in mate_copies(at, 2 * hf + n):
+                copy.wait_send()
+        for copy in chip_copies(hf):
             copy.wait_send()
-    for copy in pair_copies:
-        copy.wait_send()
-    g_copy(place, 0, mate).wait_send()
-    for n, hop in enumerate(hops):
-        g_copy(place, 1 + n, mate).wait_send()
-        g_copy(ahead(place, RING - hop, RING), 4 + n, mate).wait_send()
+        g_copy(place, 0, hf, mate).wait_send()
+        for n, hop in enumerate(hops):
+            g_copy(place, 1 + n, hf, mate).wait_send()
+            g_copy(ahead(place, RING - hop, RING), 4 + n, hf, mate).wait_send()
     loop(1, SHARDS, lambda i: p_copy(ahead(m, i, SHARDS)).wait_send())
 
 
@@ -645,9 +663,9 @@
             pltpu.VMEM((REQ * QMAX, WIDTH), bf),
             pltpu.VMEM((SHARDS, owned, WIDTH), bf),
             dma((RING,)), dma,
-            dma((3,)), dma((3,)),
-            dma((3,)), dma((3,)),
-            dma((7,)), dma((7,)),
+            dma((6,)), dma((6,)),
+            dma((6,)), dma((6,)),
+            dma((2, 7)), dma((2, 7)),
             dma((SHARDS,)), dma((SHARDS,)),
         ],
         compiler_params=pltpu.CompilerParams(

time: 155 us -> 152 us (0.981)
  Pallas kernels: 151 us -> 148 us
    pallas_call x1, Pallas kernels: 52.8 us -> 50.9 us  [merge(): pl.pallas_call(merge_kernel, out_shape=jax.ShapeDtypeStruct((REQ, TOKENS,...]
where the time goes in v5:
time: 152 us
  Pallas kernels  148 us (97%)
  local copies, waits for them, and re-layouts  2.13 us (1%)
    pallas_call x1, Pallas kernels, spread(): pl.pallas_call(spread_kernel, out_shape=(jax.ShapeDtypeStruct((PLACES, CT...  87.3 us
    pallas_call x1, Pallas kernels, merge(): pl.pallas_call(merge_kernel, out_shape=jax.ShapeDtypeStruct((REQ, TOKENS,...  50.9 us
    pallas_call x1, Pallas kernels, attend(): pl.pallas_call(attend_kernel, out_shape=(jax.ShapeDtypeStruct((REQ, ROWS,...  10 us

profile of v5, /device:TPU:1, one launch (start us, length us, event | category | flops | bytes accessed | tf_op | source)
XLA Modules:
  0.0 152.2 jit_solution(12639582209287478082)
XLA Ops:
  0.6 87.3 %spread.1 = (bf16[104,128,256]{2,1,0:T(8,128)(2,1)}, bf16[4,32,32,128]{3,2,1,0:T(8,128)(2,1)}, bf16[8,16,256]{2,1,0:T(8,128)(2,1)}, bf16[8,256,1024]{2,1,0:T(8,128)(2,1)}) custom-call(s32[8,32]{1,0:T(8,128)} %bitcast.5, bf16[16,16,2048]{2,1,0:T(8,128)(2,1)} %kv.1, bf16[4,4,8192]{2,1,0:T(4,128)(2,1)} %queries.1, bf16[4,4,2048]{2,1,0:T(4,128)(2,1)} %new_kv.1, ...), custom_call_target="tpu_custom_call" | custom-call | tf_op jit(solution)/shard_map/spread/pallas_call | solution.py:287
  87.9 0.0 copy-start.1
  87.9 10.0 %attend.1 = (bf16[4,1024,128]{2,1,0:T(8,128)(2,1)}, f32[4,8,1024]{2,1,0:T(8,128)}) custom-call(s32[8,32]{1,0:T(8,128)} %bitcast.6, s32[4,8]{1,0:T(4,128)} %places.1, s32[4]{0:T(128)} %lengths.1, f32[8,128]{1,0:T(8,128)} %constant.17.clone.cosines, f32[8,128]{1,0:T(8,128)} %constant.18.clone.sines, bf16[4,1024,128]{2,1,0:T(8,128)(2,1)} %bitcast.3, ...), custom_call_target="tpu_custom_call" | custom-call | tf_op jit(solution)/shard_map/attend/pallas_call | solution.py:417
  97.9 0.0 copy-done.1
  97.9 0.0 copy-start
  97.9 1.2 copy-done
  99.2 0.0 copy-start.2
  99.2 0.9 copy-done.2
  100.1 0.0 copy-start.3
  100.1 50.9 %merge.1 = f32[4,4,8192]{2,1,0:T(4,128)S(1)} custom-call(bf16[4,1024,128]{2,1,0:T(8,128)(2,1)S(1)} %copy-done, f32[4,8,1024]{2,1,0:T(8,128)S(1)} %copy-done.2, bf16[256,8192]{1,0:T(8,128)(2,1)} %w_own.1, bf16[8,256,1024]{2,1,0:T(8,128)(2,1)} %get-tuple-element.13.w_all, bf16[4,4,8192]{2,1,0:T(4,128)(2,1)S(1)} %copy-done.1), custom_call_target="tpu_custom_call" | custom-call | tf_op jit(solution)/shard_map/merge/pallas_call | solution.py:648
  151.0 0.2 multiply_reduce_fusion
  151.2 0.0 copy-done.3
  151.2 1.0 multiply_convert_fusion
  (2 shorter events, 0.0 us)
Async XLA Ops:
  87.9 10.0 %copy-start.1 = (bf16[4,4,8192]{2,1,0:T(4,128)(2,1)S(1)}, bf16[4,4,8192]{2,1,0:T(4,128)(2,1)}, u32[]{:S(2)}) copy-start(bf16[4,4,8192]{2,1,0:T(4,128)(2,1)} %hidden.1) | copy-start | bytes 786436
  97.9 1.2 copy-start
  99.2 0.9 copy-start.2
  100.1 51.2 %copy-start.3 = (bf16[8192]{0:T(1024)(128)(2,1)S(1)}, bf16[8192]{0:T(1024)(128)(2,1)}, u32[]{:S(2)}) copy-start(bf16[8192]{0:T(1024)(128)(2,1)} %param.21) | copy-start | bytes 49156

commit v6 on v5

--- a/solution.py
+++ b/solution.py
@@ -27,7 +27,9 @@
 CHUNKS = 4
 PART = CTOK // 4 // CHUNKS
 CAP = 8
-WINDOW = 4
+WINDOW = 6
+STEPS = 2
+STEP = HELD // STEPS
 EARLY = 3
 PLACES = 5 * HELD + 3 * CAP
 RING = 8
@@ -88,20 +90,24 @@
             src_ref=src, dst_ref=dst, send_sem=send, recv_sem=recv, device_id=where, device_id_type=MESH
         )
 
-    def kv_rows(i):
-        return kv_all.at[pl.ds(0, HELD), pl.ds(16 * i, 16), :]
-
-    def kv_part(head):
-        return kv.at[:, :, pl.ds(pl.multiple_of(2 * HD * head, 2 * HD), 2 * HD)]
-
-    def kv_copy(i):
+    def kv_rows(base, n, i):
+        return kv_all.at[pl.ds(base + STEP * n, STEP), pl.ds(16 * i, 16), :]
+
+    def kv_part(n, head):
+        return kv.at[pl.ds(STEP * n, STEP), :, pl.ds(pl.multiple_of(2 * HD * head, 2 * HD), 2 * HD)]
+
+    def kv_copy(n, i):
         to = ahead(k, KVH - i, KVH)
-        return remote(kv_part(to), kv_rows(i), kv_send.at[i], kv_recv.at[i], mp=QUARTERS * to + j)
-
-    own_kv = pltpu.make_async_copy(kv_part(k), kv_rows(0), own_sem.at[2])
-    for i in range(1, KVH):
-        kv_copy(i).start()
-    own_kv.start()
+        return remote(
+            kv_part(n, to), kv_rows(0, n, i), kv_send.at[n, i], kv_recv.at[n, i], mp=QUARTERS * to + j
+        )
+
+    def own_kv(n):
+        return pltpu.make_async_copy(kv_part(n, k), kv_rows(0, n, 0), own_sem.at[2 + n])
+
+    for n in range(STEPS):
+        for i in range(1, KVH):
+            kv_copy(n, i).start()
 
     target = (right, left)
 
@@ -111,10 +117,10 @@
     def held(base, count, c):
         return kv_all.at[pl.ds(base, count), rows_of(c)]
 
-    def z_own(way, i):
-        src = kv_part(k) if i == 0 else kv_rows(i)
-        dst = kv_all.at[pl.ds(HELD * (1 + way), HELD), pl.ds(16 * i, 16), :]
-        return remote(src, dst, o_send.at[way, i], o_recv.at[way, i], store=target[way])
+    def z_own(way, n, i):
+        src = kv_part(n, k) if i == 0 else kv_rows(0, n, i)
+        dst = kv_rows(HELD * (1 + way), n, i)
+        return remote(src, dst, o_send.at[way, n, i], o_recv.at[way, n, i], store=target[way])
 
     def z_copy(way, s, c):
         if s == 1:
@@ -180,14 +186,18 @@
         copy.start()
         sent[way].append(copy)
 
-    def push_own(i):
+    def push_own(n, i):
         if i > 0:
-            kv_copy(i).wait_recv()
+            kv_copy(n, i).wait_recv()
         for way in range(2):
-            push(way, z_own(way, i))
-
-    for i in range(EARLY):
-        push_own(i)
+            push(way, z_own(way, n, i))
+
+    for n in range(STEPS):
+        push_own(n, 0)
+    for n in range(STEPS):
+        own_kv(n).start()
+    for i in range(1, EARLY):
+        push_own(0, i)
     loop(1, RING, lambda i: w_copy(i).start())
 
     cos, sin = cosines[m], sines[m]
@@ -212,8 +222,12 @@
     loop(1, KVH, lambda i: f_copy(i).start())
     loop(1, SHARDS, lambda i: q_copy(i).start())
     for i in range(EARLY, KVH):
-        push_own(i)
-    own_kv.wait()
+        push_own(0, i)
+    for n in range(1, STEPS):
+        for i in range(1, KVH):
+            push_own(n, i)
+    for n in range(STEPS):
+        own_kv(n).wait()
 
     def wanted(dest, source):
         def look(n, carry):
@@ -235,7 +249,8 @@
     for c in range(CHUNKS):
         for way in range(2):
             for i in range(2 * c, 2 * c + 2):
-                z_own(way, i).wait_recv()
+                for n in range(STEPS):
+                    z_own(way, n, i).wait_recv()
             push(way, z_copy(way, 1, c))
 
     def keep(way, c):
@@ -274,8 +289,9 @@
     loop(1, RING, lambda i: w_copy(i).wait_send())
     loop(1, KVH, lambda i: f_copy(i).wait_send())
     loop(1, SHARDS, lambda i: q_copy(i).wait_send())
-    for i in range(1, KVH):
-        kv_copy(i).wait_send()
+    for n in range(STEPS):
+        for i in range(1, KVH):
+            kv_copy(n, i).wait_send()
     for copies in sent:
         for copy in copies[-WINDOW:]:
             copy.wait_send()
@@ -304,12 +320,12 @@
             pltpu.VMEM((2, CHUNKS // 2, CAP, PART, 2 * HD), bf),
             pltpu.VMEM((2, CHUNKS // 2, CAP, PART, 2 * HD), bf),
             dma((2, CHUNKS)),
-            dma((3,)),
-            dma((KVH,)), dma((KVH,)),
+            dma((2 + STEPS,)),
+            dma((STEPS, KVH)), dma((STEPS, KVH)),
             dma((SHARDS,)), dma((SHARDS,)),
             dma((KVH,)), dma((KVH,)),
             dma((RING,)), dma((RING,)),
-            dma((2, KVH)), dma((2, KVH)),
+            dma((2, STEPS, KVH)), dma((2, STEPS, KVH)),
             dma((2, 5, CHUNKS)), dma((2, 5, CHUNKS)),
         ],
         compiler_params=pltpu.CompilerParams(
@@ -584,7 +600,7 @@
         )
 
     def project(i):
-        block = ahead(m // per, i, 4)
+        block = ahead(m // per, i + 2, 4)
         at = block * span + lax.broadcasted_iota(jnp.int32, (span, REQ * QMAX), 0)
         source = QMAX * ((at >> 2) & 3) + 4 * (at >> 4) + (at & 3)
         pick = (source == lax.broadcasted_iota(jnp.int32, (span, REQ * QMAX), 1)).astype(jnp.bfloat16)

time: 152 us -> 148 us (0.974)
  Pallas kernels: 148 us -> 143 us
    pallas_call x1, Pallas kernels: 87.3 us -> 84.1 us  [spread(): pl.pallas_call(spread_kernel, out_shape=(jax.ShapeDtypeStruct((PLACES, CT...]
    pallas_call x1, Pallas kernels: 50.9 us -> 49.2 us  [merge(): pl.pallas_call(merge_kernel, out_shape=jax.ShapeDtypeStruct((REQ, TOKENS,...]
where the time goes in v6:
time: 148 us; the launch traced here: 147 us
  Pallas kernels  143 us (97%)
  local copies, waits for them, and re-layouts  2.13 us (1%)
    pallas_call x1, Pallas kernels, spread(): pl.pallas_call(spread_kernel, out_shape=(jax.ShapeDtypeStruct((PLACES, CT...  84.1 us
    pallas_call x1, Pallas kernels, merge(): pl.pallas_call(merge_kernel, out_shape=jax.ShapeDtypeStruct((REQ, TOKENS,...  49.2 us
    pallas_call x1, Pallas kernels, attend(): pl.pallas_call(attend_kernel, out_shape=(jax.ShapeDtypeStruct((REQ, ROWS,...  10 us

profile of v6, /device:TPU:1, one launch (start us, length us, event | category | flops | bytes accessed | tf_op | source)
XLA Modules:
  0.0 147.3 jit_solution(2904332185217865166)
XLA Ops:
  0.6 84.1 %spread.1 = (bf16[104,128,256]{2,1,0:T(8,128)(2,1)}, bf16[4,32,32,128]{3,2,1,0:T(8,128)(2,1)}, bf16[8,16,256]{2,1,0:T(8,128)(2,1)}, bf16[8,256,1024]{2,1,0:T(8,128)(2,1)}) custom-call(s32[8,32]{1,0:T(8,128)} %bitcast.5, bf16[16,16,2048]{2,1,0:T(8,128)(2,1)} %kv.1, bf16[4,4,8192]{2,1,0:T(4,128)(2,1)} %queries.1, bf16[4,4,2048]{2,1,0:T(4,128)(2,1)} %new_kv.1, ...), custom_call_target="tpu_custom_call" | custom-call | tf_op jit(solution)/shard_map/spread/pallas_call | solution.py:303
  84.8 0.0 copy-start.1
  84.8 10.0 %attend.1 = (bf16[4,1024,128]{2,1,0:T(8,128)(2,1)}, f32[4,8,1024]{2,1,0:T(8,128)}) custom-call(s32[8,32]{1,0:T(8,128)} %bitcast.6, s32[4,8]{1,0:T(4,128)} %places.1, s32[4]{0:T(128)} %lengths.1, f32[8,128]{1,0:T(8,128)} %constant.17.clone.cosines, f32[8,128]{1,0:T(8,128)} %constant.18.clone.sines, bf16[4,1024,128]{2,1,0:T(8,128)(2,1)} %bitcast.3, ...), custom_call_target="tpu_custom_call" | custom-call | tf_op jit(solution)/shard_map/attend/pallas_call | solution.py:433
  94.8 0.0 copy-done.1
  94.8 0.0 copy-start
  94.8 1.2 copy-done
  96.0 0.0 copy-start.2
  96.0 0.9 copy-done.2
  96.9 0.0 copy-start.3
  96.9 49.2 %merge.1 = f32[4,4,8192]{2,1,0:T(4,128)S(1)} custom-call(bf16[4,1024,128]{2,1,0:T(8,128)(2,1)S(1)} %copy-done, f32[4,8,1024]{2,1,0:T(8,128)S(1)} %copy-done.2, bf16[256,8192]{1,0:T(8,128)(2,1)} %w_own.1, bf16[8,256,1024]{2,1,0:T(8,128)(2,1)} %get-tuple-element.13.w_all, bf16[4,4,8192]{2,1,0:T(4,128)(2,1)S(1)} %copy-done.1), custom_call_target="tpu_custom_call" | custom-call | tf_op jit(solution)/shard_map/merge/pallas_call | solution.py:664
  146.1 0.2 multiply_reduce_fusion
  146.3 0.0 copy-done.3
  146.3 1.0 multiply_convert_fusion
  (2 shorter events, 0.0 us)
Async XLA Ops:
  84.8 10.0 %copy-start.1 = (bf16[4,4,8192]{2,1,0:T(4,128)(2,1)S(1)}, bf16[4,4,8192]{2,1,0:T(4,128)(2,1)}, u32[]{:S(2)}) copy-start(bf16[4,4,8192]{2,1,0:T(4,128)(2,1)} %hidden.1) | copy-start | bytes 786436
  94.8 1.2 copy-start
  96.0 0.9 copy-start.2
  96.9 49.4 %copy-start.3 = (bf16[8192]{0:T(1024)(128)(2,1)S(1)}, bf16[8192]{0:T(1024)(128)(2,1)}, u32[]{:S(2)}) copy-start(bf16[8192]{0:T(1024)(128)(2,1)} %param.21) | copy-start | bytes 49156

commit v7 on v6

--- a/solution.py
+++ b/solution.py
@@ -533,7 +533,7 @@
 
     other = 1 - half
     order = ((other, 0), (half, 1))
-    hops = (2, 6, 4)
+    hops = (4, 2, 6)
     mate_place = place + 1 - 2 * core
     for hf in range(2):
         for at, n in order:

time: 148 us -> 148 us (level)
  no operation moved by 1% of the time
where the time goes in v7:
time: 148 us; the launch traced here: 147 us
  Pallas kernels  143 us (97%)
  local copies, waits for them, and re-layouts  2.13 us (1%)
    pallas_call x1, Pallas kernels, spread(): pl.pallas_call(spread_kernel, out_shape=(jax.ShapeDtypeStruct((PLACES, CT...  84.1 us
    pallas_call x1, Pallas kernels, merge(): pl.pallas_call(merge_kernel, out_shape=jax.ShapeDtypeStruct((REQ, TOKENS,...  49 us
    pallas_call x1, Pallas kernels, attend(): pl.pallas_call(attend_kernel, out_shape=(jax.ShapeDtypeStruct((REQ, ROWS,...  10 us

profile of v7, /device:TPU:1, one launch (start us, length us, event | category | flops | bytes accessed | tf_op | source)
XLA Modules:
  0.0 147.2 jit_solution(15272298488590422478)
XLA Ops:
  0.6 84.1 %spread.1 = (bf16[104,128,256]{2,1,0:T(8,128)(2,1)}, bf16[4,32,32,128]{3,2,1,0:T(8,128)(2,1)}, bf16[8,16,256]{2,1,0:T(8,128)(2,1)}, bf16[8,256,1024]{2,1,0:T(8,128)(2,1)}) custom-call(s32[8,32]{1,0:T(8,128)} %bitcast.5, bf16[16,16,2048]{2,1,0:T(8,128)(2,1)} %kv.1, bf16[4,4,8192]{2,1,0:T(4,128)(2,1)} %queries.1, bf16[4,4,2048]{2,1,0:T(4,128)(2,1)} %new_kv.1, ...), custom_call_target="tpu_custom_call" | custom-call | tf_op jit(solution)/shard_map/spread/pallas_call | solution.py:303
  84.8 0.0 copy-start.1
  84.8 10.0 %attend.1 = (bf16[4,1024,128]{2,1,0:T(8,128)(2,1)}, f32[4,8,1024]{2,1,0:T(8,128)}) custom-call(s32[8,32]{1,0:T(8,128)} %bitcast.6, s32[4,8]{1,0:T(4,128)} %places.1, s32[4]{0:T(128)} %lengths.1, f32[8,128]{1,0:T(8,128)} %constant.17.clone.cosines, f32[8,128]{1,0:T(8,128)} %constant.18.clone.sines, bf16[4,1024,128]{2,1,0:T(8,128)(2,1)} %bitcast.3, ...), custom_call_target="tpu_custom_call" | custom-call | tf_op jit(solution)/shard_map/attend/pallas_call | solution.py:433
  94.8 0.0 copy-done.1
  94.8 0.0 copy-start
  94.8 1.2 copy-done
  96.0 0.0 copy-start.2
  96.0 0.9 copy-done.2
  96.9 0.0 copy-start.3
  96.9 49.0 %merge.1 = f32[4,4,8192]{2,1,0:T(4,128)S(1)} custom-call(bf16[4,1024,128]{2,1,0:T(8,128)(2,1)S(1)} %copy-done, f32[4,8,1024]{2,1,0:T(8,128)S(1)} %copy-done.2, bf16[256,8192]{1,0:T(8,128)(2,1)} %w_own.1, bf16[8,256,1024]{2,1,0:T(8,128)(2,1)} %get-tuple-element.13.w_all, bf16[4,4,8192]{2,1,0:T(4,128)(2,1)S(1)} %copy-done.1), custom_call_target="tpu_custom_call" | custom-call | tf_op jit(solution)/shard_map/merge/pallas_call | solution.py:664
  146.0 0.2 multiply_reduce_fusion
  146.2 0.0 copy-done.3
  146.2 1.0 multiply_convert_fusion
  (2 shorter events, 0.0 us)
Async XLA Ops:
  84.8 10.0 %copy-start.1 = (bf16[4,4,8192]{2,1,0:T(4,128)(2,1)S(1)}, bf16[4,4,8192]{2,1,0:T(4,128)(2,1)}, u32[]{:S(2)}) copy-start(bf16[4,4,8192]{2,1,0:T(4,128)(2,1)} %hidden.1) | copy-start | bytes 786436
  94.8 1.2 copy-start
  96.0 0.9 copy-start.2
  96.9 49.3 %copy-start.3 = (bf16[8192]{0:T(1024)(128)(2,1)S(1)}, bf16[8192]{0:T(1024)(128)(2,1)}, u32[]{:S(2)}) copy-start(bf16[8192]{0:T(1024)(128)(2,1)} %param.21) | copy-start | bytes 49156
